TPU v7x, 128 devices: a whole 4x4x4 slice. The times are simulated.
128 devices in a mesh: probe: 4 (over y_hi, core), slab: 32 (over x, y_lo, z).
Axes of the slice: x: 4, y: 4 (y_hi: 2, y_lo: 2; y = y_hi * 2 + y_lo), z: 4, core: 2. Of those that a mesh axis runs over, the one named last changes fastest.
Arguments:
- receptor: float32 [8, 256, 64, 128], P(None, 'slab'), may hold values from -14 to 14
- library: float32 [16, 8, 4913], replicated, may hold values from -1 to 1
- probe_ids: int32 [16], P('probe'), may hold values from 0 to 15, each once
- rotations: int32 [16, 1], P('probe'), may hold values from 0 to 23
- offsets: int32 [16, 1, 2], P('probe'), may hold values from 0 to 63
- probe_weight: float32 [16], replicated, may hold values from 0.25 to 4
Outputs:
- consensus: float32 [256, 64, 128], P('slab', 'probe')
Inputs may be any that keep to these rules, and one draw needn't show every extreme that they name: `probe_ids`: each probe type once. `rotations`: indices into the table ROT.
All inputs are finite; a program needn't handle non-finite values.
Results may differ from a plain program's by a relative error of at most 0.0001.
Values sent between devices are 32-bit elements; how exact they have to be, the bound alone decides.
A program may use at most 320 MiB of HBM per device.

v0:
```python
import math

import jax
import jax.numpy as jnp
import numpy as np
from jax import lax
from jax.sharding import PartitionSpec as P

RAD = 8


ENERGY_CAP = 6.0
HIGHEST = lax.Precision.HIGHEST


def with_halo(array, sides, width):
    for axis, dim in sides:
        size, length = (lax.axis_size(axis), array.shape[dim])
        up = [(i, (i + 1) % size) for i in range(size)]
        down = [(j, i) for i, j in up]
        last = lax.slice_in_dim(array, length - width, length, axis=dim)
        first = lax.slice_in_dim(array, 0, width, axis=dim)
        before = lax.ppermute(last, axis, up)
        after = lax.ppermute(first, axis, down)
        array = jnp.concatenate([before, array, after], axis=dim)
    return array


def cube_rotations():
    permutes = [(0, 1, 2), (0, 2, 1), (1, 0, 2), (1, 2, 0), (2, 0, 1), (2, 1, 0)]
    parities = [1, -1, -1, 1, 1, -1]
    tables = []
    for permute, parity in zip(permutes, parities):
        for sign_x in (1, -1):
            for sign_y in (1, -1):
                for sign_z in (1, -1):
                    if parity * sign_x * sign_y * sign_z == 1:
                        matrix = np.zeros((3, 3), np.int32)
                        sign_list = (sign_x, sign_y, sign_z)
                        for row_index in range(3):
                            matrix[row_index, permute[row_index]] = sign_list[row_index]
                        tables.append(matrix)
    return np.stack(tables)


def offset_grid(radius):
    side_len = 2 * radius + 1
    flat_index = jnp.arange(side_len**3, dtype=jnp.int32)
    return (
        flat_index // (side_len * side_len) - radius,
        flat_index // side_len % side_len - radius,
        flat_index % side_len - radius,
    )


def rotated_kernel(library, type_id, rot_id, radius):
    side_len = 2 * radius + 1
    turning = jnp.asarray(cube_rotations())[rot_id]
    step_x, step_y, step_z = offset_grid(radius)
    moved_to = [
        turning[row_index, 0] * step_x
        + turning[row_index, 1] * step_y
        + turning[row_index, 2] * step_z
        + radius
        for row_index in range(3)
    ]
    source = (moved_to[0] * side_len + moved_to[1]) * side_len + moved_to[2]
    return jnp.take(library[type_id], source, axis=1)


def phase_tables(points, length):
    frequency = jnp.arange(length, dtype=jnp.int32)
    wrapped = points[:, None] * frequency[None, :] % length
    angles = wrapped.astype(jnp.float32) * (2.0 * math.pi / length)
    return (jnp.cos(angles), jnp.sin(angles))


def turn_complex(form, real_in, imag_in, cosine_table, sine_table, direction):
    real_out = jnp.einsum(form, real_in, cosine_table, precision=HIGHEST) - direction * jnp.einsum(
        form, imag_in, sine_table, precision=HIGHEST
    )
    imag_out = jnp.einsum(form, imag_in, cosine_table, precision=HIGHEST) + direction * jnp.einsum(
        form, real_in, sine_table, precision=HIGHEST
    )
    return (real_out, imag_out)


def spectrum_yz(grid_values):
    plane_count = grid_values.shape[2]
    row_count = grid_values.shape[3]
    cosine_rows, sine_rows = phase_tables(jnp.arange(row_count, dtype=jnp.int32), row_count)
    real_rows = jnp.einsum("txzy,yk->txzk", grid_values, cosine_rows, precision=HIGHEST)
    imag_rows = -jnp.einsum("txzy,yk->txzk", grid_values, sine_rows, precision=HIGHEST)
    cosine_depth, sine_depth = phase_tables(jnp.arange(plane_count, dtype=jnp.int32), plane_count)
    return turn_complex("txzy,zk->txky", real_rows, imag_rows, cosine_depth, sine_depth, -1.0)


def kernel_spectrum(kernel, radius, extended, plane_count, row_count):
    side_len = 2 * radius + 1
    cube = kernel.reshape(kernel.shape[0], side_len, side_len, side_len)
    steps = jnp.arange(side_len, dtype=jnp.int32) - radius
    cosine_across, sine_across = phase_tables(steps, extended)
    real_across = jnp.einsum("tabc,ak->tkbc", cube, cosine_across, precision=HIGHEST)
    imag_across = jnp.einsum("tabc,ak->tkbc", cube, sine_across, precision=HIGHEST)
    cosine_depth, sine_depth = phase_tables(steps, plane_count)
    real_depth, imag_depth = turn_complex(
        "tkbc,cj->tkbj", real_across, imag_across, cosine_depth, sine_depth, 1.0
    )
    cosine_rows, sine_rows = phase_tables(steps, row_count)
    return turn_complex("tkbj,bm->tkjm", real_depth, imag_depth, cosine_rows, sine_rows, 1.0)


def energy_map(joint_real, joint_imag, radius, slab_planes):
    extended, plane_count, row_count = joint_real.shape
    cosine_out, sine_out = phase_tables(
        jnp.arange(radius, radius + slab_planes, dtype=jnp.int32), extended
    )
    real_across, imag_across = turn_complex(
        "kzy,nk->nzy", joint_real, joint_imag, cosine_out, sine_out, 1.0
    )
    cosine_depth, sine_depth = phase_tables(jnp.arange(plane_count, dtype=jnp.int32), plane_count)
    real_depth, imag_depth = turn_complex(
        "nky,jk->njy", real_across, imag_across, cosine_depth, sine_depth, 1.0
    )
    cosine_rows, sine_rows = phase_tables(jnp.arange(row_count, dtype=jnp.int32), row_count)
    real_rows = jnp.einsum("njk,mk->njm", real_depth, cosine_rows, precision=HIGHEST) - jnp.einsum(
        "njk,mk->njm", imag_depth, sine_rows, precision=HIGHEST
    )
    return real_rows / (extended * plane_count * row_count)


def smooth_rolled(values_in, axis_index):
    return (
        jnp.roll(values_in, 1, axis_index) + 2.0 * values_in + jnp.roll(values_in, -1, axis_index)
    ) * 0.25


def smooth_sliced(values_in, axis_index):
    length = values_in.shape[axis_index]
    lower = lax.slice_in_dim(values_in, 0, length - 2, axis=axis_index)
    middle = lax.slice_in_dim(values_in, 1, length - 1, axis=axis_index)
    upper = lax.slice_in_dim(values_in, 2, length, axis=axis_index)
    return (lower + 2.0 * middle + upper) * 0.25


def local(receptor, library, probe_ids, rotations, offsets, probe_weight):
    term_count, slab_planes, plane_count, row_count = receptor.shape
    radius = RAD
    extended = slab_planes + 2 * radius
    slab_devices = lax.axis_size("slab")
    total_cells = slab_planes * slab_devices * plane_count * row_count
    widened = with_halo(receptor, (("slab", 1),), radius)
    real_yz, imag_yz = spectrum_yz(widened)
    cosine_slab, sine_slab = phase_tables(jnp.arange(extended, dtype=jnp.int32), extended)
    grid_real, grid_imag = turn_complex(
        "txzy,xk->tkzy", real_yz, imag_yz, cosine_slab, sine_slab, -1.0
    )
    slot_count = probe_ids.shape[0]
    totals = []
    for slot_index in range(slot_count):
        kernel = rotated_kernel(library, probe_ids[slot_index], rotations[slot_index, 0], radius)
        probe_real, probe_imag = kernel_spectrum(kernel, radius, extended, plane_count, row_count)
        joint_real = jnp.einsum(
            "tkzy,tkzy->kzy", grid_real, probe_real, precision=HIGHEST
        ) - jnp.einsum("tkzy,tkzy->kzy", grid_imag, probe_imag, precision=HIGHEST)
        joint_imag = jnp.einsum(
            "tkzy,tkzy->kzy", grid_real, probe_imag, precision=HIGHEST
        ) + jnp.einsum("tkzy,tkzy->kzy", grid_imag, probe_real, precision=HIGHEST)
        energy = energy_map(joint_real, joint_imag, radius, slab_planes)
        energy = jnp.roll(
            energy, (offsets[slot_index, 0, 1], offsets[slot_index, 0, 0]), axis=(1, 2)
        )
        total = jnp.exp(-ENERGY_CAP * jnp.tanh(energy / ENERGY_CAP))
        totals.append(total)
    partition = lax.psum(jnp.stack([jnp.sum(total) for total in totals]), "slab")
    type_count = probe_weight.shape[0]
    onehot = (probe_ids[:, None] == jnp.arange(type_count, dtype=jnp.int32)[None, :]).astype(
        jnp.float32
    )
    chosen = jnp.dot(onehot, probe_weight, precision=HIGHEST)
    mixture = jnp.zeros((slab_planes, plane_count, row_count), jnp.float32)
    for slot_index in range(slot_count):
        mixture = mixture + chosen[slot_index] * (
            total_cells * totals[slot_index] / partition[slot_index]
        )
    widened_sum = with_halo(mixture, (("slab", 0),), 1)
    local_smooth = smooth_rolled(smooth_rolled(smooth_sliced(widened_sum, 0), 1), 2)
    smoothed = lax.psum_scatter(local_smooth, "probe", scatter_dimension=1, tiled=True)
    return smoothed / type_count


def solution(mesh):
    in_specs = (
        P(None, "slab", None, None),
        P(),
        P("probe"),
        P("probe", None),
        P("probe", None, None),
        P(),
    )
    out_specs = P("slab", "probe", None)
    return jax.shard_map(local, mesh=mesh, in_specs=in_specs, out_specs=out_specs, check_vma=False)
```

profile of v0, /device:TPU:1, one launch (start us, length us, event | category | flops | bytes accessed | tf_op | source)
XLA Modules:
  0.0 688.6 jit_solution(821175243983087067)
XLA Ops:
  6.5 2.5 collective-permute-start
  9.0 5.3 collective-permute-start.1
  31.0 5.7 compare_select_fusion
  36.7 5.7 compare_and_fusion
  46.9 10.1 %gather_fusion.3 = f32[4913,8]{1,0:T(8,128)} fusion(f32[8,4913]{0,1:T(8,128)S(1)} %bitcast.485, s32[5120]{0:T(1024)S(1)} %pad_clamp_fusion), kind=kCustom, calls=%fused_computation.3.clone | custom fusion | bytes 334084 | tf_op jit(solution)/shard_map/jit(_take)/gather | solution.py:68
  57.0 3.9 select_bitcast_fusion
  62.2 1.6 fusion.84
  68.6 12.1 %fusion.20 = f32[8,24,64,128]{3,2,1,0:T(8,128)} fusion(f32[8,24,17,64]{3,1,2,0:T(8,128)S(1)} %fusion.121, s32[17]{0:T(128)S(1)} %iota_add_fusion), kind=kOutput, calls=%fused_computation.36 | convolution fusion | flops 320894720 | bytes 7127108 | tf_op jit(solution)/shard_map/tkbj,bm->tkjm/dot_general | solution.py:82
  80.7 12.2 %fusion.22 = f32[8,24,64,128]{3,2,1,0:T(8,128)} fusion(f32[8,24,17,64]{3,1,2,0:T(8,128)S(1)} %fusion.121, s32[17]{0:T(128)S(1)} %iota_add_fusion), kind=kOutput, calls=%fused_computation.38 | convolution fusion | flops 320894720 | bytes 7127108 | tf_op jit(solution)/shard_map/tkbj,bm->tkjm/dot_general | solution.py:79
  92.8 2.8 fusion.54
  95.6 5.7 compare_select_fusion.1
  101.3 5.7 compare_and_fusion.1
  107.7 10.1 %gather_fusion.2 = f32[4913,8]{1,0:T(8,128)} fusion(f32[8,4913]{0,1:T(8,128)S(1)} %bitcast.486, s32[5120]{0:T(1024)S(1)} %pad_clamp_fusion.1), kind=kCustom, calls=%fused_computation.2.clone | custom fusion | bytes 334084 | tf_op jit(solution)/shard_map/jit(_take)/gather | solution.py:68
  117.8 3.9 select_bitcast_fusion.1
  123.1 1.6 fusion.88
  129.4 12.4 %fusion.28 = f32[8,24,64,128]{3,2,1,0:T(8,128)} fusion(f32[8,24,17,64]{3,1,2,0:T(8,128)S(1)} %fusion.115, s32[17]{0:T(128)S(1)} %iota_add_fusion), kind=kOutput, calls=%fused_computation.44 | convolution fusion | flops 320894720 | bytes 7127108 | tf_op jit(solution)/shard_map/tkbj,bm->tkjm/dot_general | solution.py:82
  141.8 12.1 %fusion.30 = f32[8,24,64,128]{3,2,1,0:T(8,128)} fusion(f32[8,24,17,64]{3,1,2,0:T(8,128)S(1)} %fusion.115, s32[17]{0:T(128)S(1)} %iota_add_fusion), kind=kOutput, calls=%fused_computation.46 | convolution fusion | flops 320894720 | bytes 7127108 | tf_op jit(solution)/shard_map/tkbj,bm->tkjm/dot_general | solution.py:79
  157.0 12.0 %fusion.32 = f32[8,24,64,128]{3,2,1,0:T(8,128)} fusion(f32[8,24,17,64]{3,1,2,0:T(8,128)S(1)} %fusion.112, s32[17]{0:T(128)S(1)} %iota_add_fusion), kind=kOutput, calls=%fused_computation.48 | convolution fusion | flops 320894720 | bytes 7127108 | tf_op jit(solution)/shard_map/tkbj,bm->tkjm/dot_general | solution.py:82
  169.1 12.1 %fusion.34 = f32[8,24,64,128]{3,2,1,0:T(8,128)} fusion(f32[8,24,17,64]{3,1,2,0:T(8,128)S(1)} %fusion.112, s32[17]{0:T(128)S(1)} %iota_add_fusion), kind=kOutput, calls=%fused_computation.50 | convolution fusion | flops 320894720 | bytes 7127108 | tf_op jit(solution)/shard_map/tkbj,bm->tkjm/dot_general | solution.py:79
  181.9 5.6 compare_select_fusion.2
  187.5 5.6 compare_and_fusion.2
  193.8 10.1 %gather_fusion.1 = f32[4913,8]{1,0:T(8,128)} fusion(f32[8,4913]{0,1:T(8,128)S(1)} %bitcast.487, s32[5120]{0:T(1024)S(1)} %pad_clamp_fusion.2), kind=kCustom, calls=%fused_computation.1.clone | custom fusion | bytes 334084 | tf_op jit(solution)/shard_map/jit(_take)/gather | solution.py:68
  203.9 4.2 select_bitcast_fusion.2
  209.4 1.6 fusion.92
  215.7 12.4 %fusion.36 = f32[8,24,64,128]{3,2,1,0:T(8,128)} fusion(f32[8,24,17,64]{3,1,2,0:T(8,128)S(1)} %fusion.109, s32[17]{0:T(128)S(1)} %iota_add_fusion), kind=kOutput, calls=%fused_computation.52 | convolution fusion | flops 320894720 | bytes 7127108 | tf_op jit(solution)/shard_map/tkbj,bm->tkjm/dot_general | solution.py:82
  228.1 12.0 %fusion.38 = f32[8,24,64,128]{3,2,1,0:T(8,128)} fusion(f32[8,24,17,64]{3,1,2,0:T(8,128)S(1)} %fusion.109, s32[17]{0:T(128)S(1)} %iota_add_fusion), kind=kOutput, calls=%fused_computation.54 | convolution fusion | flops 320894720 | bytes 7127108 | tf_op jit(solution)/shard_map/tkbj,bm->tkjm/dot_general | solution.py:79
  243.3 11.9 %fusion.40 = f32[8,24,64,128]{3,2,1,0:T(8,128)} fusion(f32[8,24,17,64]{3,1,2,0:T(8,128)S(1)} %fusion.106, s32[17]{0:T(128)S(1)} %iota_add_fusion), kind=kOutput, calls=%fused_computation.56 | convolution fusion | flops 320894720 | bytes 7127108 | tf_op jit(solution)/shard_map/tkbj,bm->tkjm/dot_general | solution.py:82
  255.2 12.1 %fusion.42 = f32[8,24,64,128]{3,2,1,0:T(8,128)} fusion(f32[8,24,17,64]{3,1,2,0:T(8,128)S(1)} %fusion.106, s32[17]{0:T(128)S(1)} %iota_add_fusion), kind=kOutput, calls=%fused_computation.58 | convolution fusion | flops 320894720 | bytes 7127108 | tf_op jit(solution)/shard_map/tkbj,bm->tkjm/dot_general | solution.py:79
  267.3 5.6 compare_select_fusion.3
  272.9 5.6 compare_and_fusion.3
  279.2 10.1 %gather_fusion = f32[4913,8]{1,0:T(8,128)} fusion(f32[8,4913]{0,1:T(8,128)S(1)} %bitcast.488, s32[5120]{0:T(1024)S(1)} %pad_clamp_fusion.3), kind=kCustom, calls=%fused_computation.clone | custom fusion | bytes 334084 | tf_op jit(solution)/shard_map/jit(_take)/gather | solution.py:68
  289.3 4.2 select_bitcast_fusion.3
  294.7 1.6 fusion.96
  296.3 2.8 fusion.98
  299.1 2.8 fusion.76
  301.9 2.8 fusion.78
  320.6 3.3 fusion.118
  323.9 1.6 fusion.103
  325.5 12.4 %fusion.44 = f32[8,24,64,128]{3,2,1,0:T(8,128)} fusion(f32[8,24,17,64]{3,1,2,0:T(8,128)S(1)} %fusion.103, s32[17]{0:T(128)S(1)} %iota_add_fusion), kind=kOutput, calls=%fused_computation.60 | convolution fusion | flops 320894720 | bytes 7127108 | tf_op jit(solution)/shard_map/tkbj,bm->tkjm/dot_general | solution.py:82
  338.1 3.5 fusion.100
  341.7 12.3 %fusion.46 = f32[8,24,64,128]{3,2,1,0:T(8,128)} fusion(f32[8,24,17,64]{3,1,2,0:T(8,128)S(1)} %fusion.103, s32[17]{0:T(128)S(1)} %iota_add_fusion), kind=kOutput, calls=%fused_computation.62 | convolution fusion | flops 320894720 | bytes 7127108 | tf_op jit(solution)/shard_map/tkbj,bm->tkjm/dot_general | solution.py:79
  353.9 11.9 %fusion.48 = f32[8,24,64,128]{3,2,1,0:T(8,128)} fusion(f32[8,24,17,64]{3,1,2,0:T(8,128)S(1)} %fusion.100, s32[17]{0:T(128)S(1)} %iota_add_fusion), kind=kOutput, calls=%fused_computation.64 | convolution fusion | flops 320894720 | bytes 7127108 | tf_op jit(solution)/shard_map/tkbj,bm->tkjm/dot_general | solution.py:82
  365.8 12.1 %fusion.50 = f32[8,24,64,128]{3,2,1,0:T(8,128)} fusion(f32[8,24,17,64]{3,1,2,0:T(8,128)S(1)} %fusion.100, s32[17]{0:T(128)S(1)} %iota_add_fusion), kind=kOutput, calls=%fused_computation.66 | convolution fusion | flops 320894720 | bytes 7127108 | tf_op jit(solution)/shard_map/tkbj,bm->tkjm/dot_general | solution.py:79
  377.9 12.3 %fusion.24 = f32[8,24,64,128]{3,2,1,0:T(8,128)} fusion(f32[8,24,17,64]{3,1,2,0:T(8,128)S(1)} %fusion.118, s32[17]{0:T(128)S(1)} %iota_add_fusion), kind=kOutput, calls=%fused_computation.40 | convolution fusion | flops 320894720 | bytes 7127108 | tf_op jit(solution)/shard_map/tkbj,bm->tkjm/dot_general | solution.py:82
  390.3 1.9 constant_dynamic-update-slice_fusion.2
  392.7 1.7 constant_dynamic-update-slice_fusion
  394.4 5.3 fusion.202
  399.7 5.3 fusion.200
  405.0 6.0 fusion.234
  411.1 5.8 fusion.230
  416.9 6.3 add_bitcast_fusion.1
  423.2 9.0 %fusion.2 = f32[24,8,64,128]{3,0,2,1:T(8,128)S(1)} fusion(f32[8,24,64,128]{3,2,1,0:T(8,128)S(1)} %add_bitcast_fusion.1), kind=kOutput, calls=%fused_computation.26 | convolution fusion | flops 452990016 | bytes 12582912 | tf_op jit(solution)/shard_map/txzy,xk->tkzy/dot_general | solution.py:79
  432.1 8.5 %fusion = f32[24,8,64,128]{3,0,2,1:T(8,128)S(1)} fusion(f32[8,24,64,128]{3,2,1,0:T(8,128)S(1)} %add_bitcast_fusion.1), kind=kOutput, calls=%fused_computation.24 | convolution fusion | flops 452990016 | bytes 12582912 | tf_op jit(solution)/shard_map/txzy,xk->tkzy/dot_general | solution.py:82
  440.7 6.3 subtract_bitcast_fusion.1
  447.0 9.6 %subtract_bitcast_fusion = f32[24,64,128,8]{2,0,1,3:T(8,128)} fusion(f32[24,8,64,128]{3,0,2,1:T(8,128)S(1)} %fusion.2, f32[8,24,64,128]{3,2,1,0:T(8,128)S(1)} %subtract_bitcast_fusion.1), kind=kOutput, calls=%fused_computation.21 | convolution fusion | flops 456135744 | bytes 18874368 | tf_op jit(solution)/shard_map/txzy,xk->tkzy/dot_general | solution.py:79
  456.6 9.8 %add_bitcast_fusion = f32[24,64,128,8]{2,0,1,3:T(8,128)} fusion(f32[24,8,64,128]{3,0,2,1:T(8,128)S(1)} %fusion, f32[8,24,64,128]{3,2,1,0:T(8,128)S(1)} %subtract_bitcast_fusion.1), kind=kOutput, calls=%fused_computation.20 | convolution fusion | flops 456135744 | bytes 18874368 | tf_op jit(solution)/shard_map/txzy,xk->tkzy/dot_general | solution.py:82
  466.4 43.1 %multiply_reduce_fusion = (f32[24,64,128]{2,1,0:T(8,128)S(1)}, f32[24,64,128]{2,1,0:T(8,128)}, f32[24,64,128]{2,1,0:T(8,128)}, f32[24,64,128]{2,1,0:T(8,128)}, f...) fusion(f32[24,64,128,8]{2,0,1,3:T(8,128)} %add_bitcast_fusion, ...), kind=kOutput, calls=%fused_computation.4 | convolution fusion | flops 380663552 | bytes 120373312 | tf_op jit(solution)/shard_map/tkbj,bm->tkjm/dot_general | solution.py:79
  509.5 2.9 fusion.166
  522.9 1.7 convolution_add_fusion.5
  553.6 2.6 pad_maximum_fusion.2
  556.8 64.8 %psum.7 = f32[4]{0:T(128)S(1)} all-reduce(f32[4]{0:T(128)S(1)} %pad_maximum_fusion.2), channel_id=1, replica_groups=mesh['probe'=4,'slab'=32] {'slab'}, use_global_device_ids=true, to_apply=%region_4.7 | all-reduce | flops 4 | bytes 32 | tf_op jit(solution)/shard_map/psum | solution.py:175
  622.2 5.6 multiply_add_fusion
  627.9 5.7 collective-permute-start.3
  636.3 43.5 %reduce-scatter.2.cloned.1.call-done = f32[8,16,128]{2,1,0:T(8,128)} async-done(((f32[8,64,128]{2,1,0:T(8,128)}), f32[8,16,128]{2,1,0:T(8,128)}) %reduce-scatter.2.cloned.1.call-update) | async-done | bytes 65552 | tf_op jit(solution)/shard_map/reduce_scatter | solution.py:188
  (150 shorter events, 80.5 us)
Async XLA Ops:
  6.5 331.4 %copy-start = (f32[16]{0:T(128)S(1)}, f32[16]{0:T(128)}, u32[]{:S(2)}) copy-start(f32[16]{0:T(128)} %param.19) | copy-start | bytes 196
  6.5 673.3 %reduce-scatter.2.cloned.1.call-start = ((), (), s32[]{:S(2)}) async-start(), calls=%async_computation.1 | async-start | bytes 327680 | tf_op jit(solution)/shard_map/reduce_scatter | solution.py:188
  6.5 383.7 %collective-permute-start = (f32[8,8,64,128]{3,2,1,0:T(8,128)}, f32[8,8,64,128]{3,2,1,0:T(8,128)}, u32[]{:S(2)}, u32[]{:S(2)}) collective-permute-start(f32[8,8,64,128]{3,2,1,0:T(8,128)} %param.14), channel_id=1, source_target_pairs={{0,1},{1,2},{2,3},{3,4},{4,5},{5,6},{6,7},{7,8},{8,9},{9,10},{10,1... | collective-permute-start | bytes 6291464 | tf_op jit(solution)/shard_map/ppermute | solution.py:23
  9.0 383.7 %collective-permute-start.1 = (f32[8,8,64,128]{3,2,1,0:T(8,128)}, f32[8,8,64,128]{3,2,1,0:T(8,128)}, u32[]{:S(2)}, u32[]{:S(2)}) collective-permute-start(f32[8,8,64,128]{3,2,1,0:T(8,128)} %param.14), channel_id=1, source_target_pairs={{1,0},{2,1},{3,2},{4,3},{5,4},{6,5},{7,6},{8,7},{9,8},{10,9},{11,1... | collective-permute-start | bytes 6291464 | tf_op jit(solution)/shard_map/ppermute | solution.py:24
  65.4 3.2 copy-start.2
  301.9 2.8 copy-start.21
  301.9 18.6 %copy-start.3 = (f32[24,8,17,17]{3,0,2,1:T(8,128)S(1)}, f32[24,8,17,17]{3,0,2,1:T(8,128)}, u32[]{:S(2)}) copy-start(f32[24,8,17,17]{3,0,2,1:T(8,128)} %copy-done.2) | copy-start | bytes 665860
  320.6 3.3 copy-start.4
  320.6 3.3 copy-start.19
  325.5 12.4 %copy-start.22 = (s32[4]{0:T(128)S(1)}, s32[4]{0:T(128)}, u32[]{:S(2)}) copy-start(s32[4]{0:T(128)} %param.16) | copy-start | bytes 52
  390.2 2.2 copy-start.20
  509.5 2.9 copy-start.17
  509.5 2.9 copy-start.18
  512.4 3.6 copy-start.15
  512.4 3.6 copy-start.16
  516.0 3.8 copy-start.11
  516.0 3.8 copy-start.12
  517.5 3.8 copy-start.13
  517.6 3.8 copy-start.14
  525.1 3.8 copy-start.7
  525.2 3.8 copy-start.8
  526.7 3.8 copy-start.9
  526.7 3.8 copy-start.10
  535.6 4.0 copy-start.5
  535.6 4.0 copy-start.6
  627.8 7.1 %collective-permute-start.2 = (f32[1,64,128]{2,1,0:T(8,128)S(1)}, f32[1,64,128]{2,1,0:T(8,128)S(1)}, u32[]{:S(2)}, u32[]{:S(2)}) collective-permute-start(f32[1,64,128]{2,1,0:T(8,128)S(1)} %get-tuple-element.93), channel_id=1, source_target_pairs={{0,1},{1,2},{2,3},{3,4},{4,5},{5,6},{6,7},{7,8},{8,9},{9,10},{10,1... | collective-permute-start | bytes 98312 | tf_op jit(solution)/shard_map/ppermute | solution.py:23
  627.9 7.0 %collective-permute-start.3 = (f32[1,64,128]{2,1,0:T(8,128)S(1)}, f32[1,64,128]{2,1,0:T(8,128)S(1)}, u32[]{:S(2)}, u32[]{:S(2)}) collective-permute-start(f32[1,64,128]{2,1,0:T(8,128)S(1)} %get-tuple-element.94), channel_id=1, source_target_pairs={{1,0},{2,1},{3,2},{4,3},{5,4},{6,5},{7,6},{8,7},{9,8},{10,9},{11,1... | collective-permute-start | bytes 98312 | tf_op jit(solution)/shard_map/ppermute | solution.py:24
  635.0 46.3 %copy-start.1 = (f32[16]{0:T(128)S(1)}, f32[16]{0:T(128)}, u32[]{:S(2)}) copy-start(f32[16]{0:T(128)} %param.19) | copy-start | bytes 196
Sparse Core Ops, SparseCore 0:
  636.4 43.3 reduce-scatter.1
where the time goes:
time: 698 us; the launch traced here: 689 us
  matrix products  383 us (55%)
  other arithmetic  75.9 us (11%)
  blocking collectives  64.8 us (9%)
  local copies, waits for them, and re-layouts  61.1 us (9%)
  between operations  45 us (6%)
  waiting for transfers between devices  44.8 us (6%)
  starting transfers between devices  13.5 us (2%)
    dot_general x18, matrix products, turn_complex(): jnp.einsum(form, real_in, cosine_table, precision=HIGHEST)  113 us
    dot_general x18, matrix products, turn_complex(): jnp.einsum(form, imag_in, cosine_table, precision=HIGHEST)  81.1 us
    dot_general x18, matrix products, turn_complex(): jnp.einsum(form, imag_in, sine_table, precision=HIGHEST)  80.6 us
    dot_general x18, matrix products, turn_complex(): jnp.einsum(form, real_in, sine_table, precision=HIGHEST)  78.6 us
    psum x1, blocking collectives, local(): lax.psum(jnp.stack([jnp.sum(total) for total in totals]), 'slab')  64.8 us
    reduce_scatter x1, waiting for transfers between devices, local(): lax.psum_scatter(local_smooth, 'probe', scatter_dimension=1, tiled=True)  43.5 us
    gather x4, local copies, waits for them, and re-layouts, rotated_kernel(): return jnp.take(library[type_id], source, axis=1)  40.4 us
    select_n x8, other arithmetic, rotated_kernel(): return jnp.take(library[type_id], source, axis=1)  38.8 us
  transfers between devices with their start and end apart: 5, of which 2 were waited for; matrix products, arithmetic and copies ran while one was open for 50% of the time, Pallas kernels for 0%

commit v1 on v0

v1 whole, which is shorter than its diff:
```python
import functools
import math

import jax
import jax.numpy as jnp
import ml_dtypes
import numpy as np
from jax import lax
from jax.experimental import pallas as pl
from jax.experimental.pallas import tpu as pltpu
from jax.sharding import PartitionSpec as P

RAD = 8
KS = 17
AZ = 24
EXT = 24
KX = 13
PAIRS = 7
NZ = 64
NY = 128
ENERGY_CAP = 6.0
HIGHEST = lax.Precision.HIGHEST
MESH = pl.DeviceIdType.MESH
BF = jnp.bfloat16
F32 = jnp.float32


def cube_rotations():
    permutes = [(0, 1, 2), (0, 2, 1), (1, 0, 2), (1, 2, 0), (2, 0, 1), (2, 1, 0)]
    parities = [1, -1, -1, 1, 1, -1]
    perms, signs = [], []
    for permute, parity in zip(permutes, parities):
        for sign_x in (1, -1):
            for sign_y in (1, -1):
                for sign_z in (1, -1):
                    if parity * sign_x * sign_y * sign_z == 1:
                        perms.append(permute)
                        signs.append((sign_x, sign_y, sign_z))
    return np.array(perms, np.int32), np.array(signs, np.int32)


def split_np(table):
    table = table.astype(np.float32)
    hi = table.astype(ml_dtypes.bfloat16)
    lo = (table - hi.astype(np.float32)).astype(ml_dtypes.bfloat16)
    return hi, lo


def xy_table():
    a = np.arange(KS) - RAD
    kx = np.arange(2 * PAIRS)
    ky = np.arange(NY)
    px = (a[:, None] * kx[None, :]) % EXT / EXT
    py = (a[:, None] * ky[None, :]) % NY / NY
    ang = 2 * np.pi * (px[:, None, :, None] + py[None, :, None, :])
    live = (kx < KX).astype(np.float64)[None, None, :, None]
    both = np.stack([np.cos(ang) * live, np.sin(ang) * live], axis=2)
    both = both.reshape(KS, KS, 2, PAIRS, 2, NY).transpose(0, 1, 3, 2, 4, 5)
    return both.reshape(KS * KS, PAIRS * 2 * 2 * NY)


def probe_z_table():
    a = np.arange(AZ) - RAD
    live = (np.arange(AZ) < KS).astype(np.float64)
    kz = np.arange(NZ)
    ang = 2 * np.pi * ((kz[:, None] * a[None, :]) % NZ) / NZ
    c, s = np.cos(ang) * live, np.sin(ang) * live
    t = np.block([[c, -s], [s, c]])
    hi, lo = split_np(t)
    return np.concatenate([hi, lo, hi], axis=1)


def grid_z_table():
    k = np.arange(NZ)
    ang = 2 * np.pi * ((k[:, None] * k[None, :]) % NZ) / NZ
    t = np.concatenate([np.cos(ang), np.sin(ang)], axis=0)
    hi, lo = split_np(t)
    return np.concatenate([hi, lo, hi], axis=1)


def grid_y_table(direction):
    k = np.arange(NY)
    ang = 2 * np.pi * ((k[:, None] * k[None, :]) % NY) / NY
    c, s = np.cos(ang), direction * np.sin(ang)
    return split_np(np.block([[c, s], [-s, c]]))


def split(x):
    hi = x.astype(BF)
    lo = (x - hi.astype(F32)).astype(BF)
    return hi, lo


def probe_kernel(tz_ref, y_ref, q_ref):
    tz = tz_ref[...]
    for p in range(PAIRS):
        d = jnp.concatenate(
            [y_ref[0, :, p * 512 : p * 512 + 256], y_ref[0, :, p * 512 + 256 : p * 512 + 512]], axis=0
        )
        hi, lo = split(d)
        rhs = jnp.concatenate([hi, hi, lo], axis=0)
        q_ref[0, p] = jnp.dot(tz, rhs, preferred_element_type=F32)


def cos24(m):
    return math.cos(2 * math.pi * (m % 24) / 24)


def sin24(m):
    return math.sin(2 * math.pi * (m % 24) / 24)


def lin(terms):
    total = None
    for coef, value in terms:
        if abs(coef) < 1e-12:
            continue
        if abs(coef - 1) < 1e-12:
            total = value if total is None else total + value
        elif abs(coef + 1) < 1e-12:
            total = -value if total is None else total - value
        else:
            total = coef * value if total is None else total + coef * value
    return total


def real_dft24(r):
    a = [r[0]] + [r[n] + r[24 - n] for n in range(1, 12)] + [r[12]]
    b = [None] + [r[n] - r[24 - n] for n in range(1, 12)]
    re, im = [None] * 13, [None] * 13
    c = [a[n] + a[12 - n] for n in range(6)] + [a[6]]
    d = [a[n] - a[12 - n] for n in range(6)]
    ce = [c[n] + c[6 - n] for n in range(3)] + [c[3]]
    co = [c[n] - c[6 - n] for n in range(3)]
    for m in range(7):
        if m % 2 == 0:
            re[2 * m] = lin([(cos24(2 * m * n), ce[n]) for n in range(4)])
        else:
            re[2 * m] = lin([(cos24(2 * m * n), co[n]) for n in range(3)])
    for k in range(1, 12, 2):
        re[k] = lin([(cos24(k * n), d[n]) for n in range(6)])
    e = [None] + [b[n] + b[12 - n] for n in range(1, 6)] + [b[6]]
    f = [None] + [b[n] - b[12 - n] for n in range(1, 6)]
    for k in range(1, 12, 2):
        im[k] = lin([(-sin24(k * n), e[n]) for n in range(1, 7)])
    fo = [None] + [f[n] + f[6 - n] for n in range(1, 3)] + [f[3]]
    fe = [None] + [f[n] - f[6 - n] for n in range(1, 3)]
    for m in range(1, 6):
        if m % 2 == 1:
            im[2 * m] = lin([(-sin24(2 * m * n), fo[n]) for n in range(1, 4)])
        else:
            im[2 * m] = lin([(-sin24(2 * m * n), fe[n]) for n in range(1, 3)])
    return re, im


def y_stage(x, w_hi, w_lo):
    hi, lo = split(x)
    out = jnp.dot(hi, w_hi, preferred_element_type=F32)
    out = out + jnp.dot(lo, w_hi, preferred_element_type=F32)
    return out + jnp.dot(hi, w_lo, preferred_element_type=F32)


def z_stage(tz, x, direction):
    hi, lo = split(x)
    rhs = jnp.concatenate([hi, hi, lo], axis=0)
    p = jnp.dot(tz, rhs, preferred_element_type=F32)
    re = p[:NZ, :NY] - direction * p[NZ:, NY:]
    im = p[:NZ, NY:] + direction * p[NZ:, :NY]
    return re, im


def energy_kernel(
    scalars,
    own_ref,
    before_a,
    before_b,
    after_a,
    after_b,
    q_ref,
    tz_ref,
    wf_hi,
    wf_lo,
    wi_hi,
    wi_lo,
    total_ref,
    sum_ref,
    spec,
    work,
):
    step = pl.program_id(0)
    tz = tz_ref[...]

    def forward(before_ref, after_ref):
        @pl.loop(0, 8)
        def _(chunk):
            rows = pl.ds(pl.multiple_of(chunk * 8, 8), 8)
            r = (
                [before_ref[0, n, rows] for n in range(8)]
                + [own_ref[0, n, rows] for n in range(8)]
                + [after_ref[0, n, rows] for n in range(8)]
            )
            re, im = real_dft24(r)
            for k in range(KX):
                work[k, rows, :NY] = re[k]
                work[k, rows, NY:] = im[k] if im[k] is not None else jnp.zeros_like(re[k])

        @pl.loop(0, KX)
        def _(k):
            y = y_stage(work[k], wf_hi[...], wf_lo[...])
            re, im = z_stage(tz, y, -1.0)
            spec[step, k, :, :NY] = re
            spec[step, k, :, NY:] = im

    @pl.when(step < 4)
    def _():
        forward(before_a, after_a)

    @pl.when((step >= 4) & (step < 8))
    def _():
        forward(before_b, after_b)

    @pl.when(step >= 8)
    def _():
        slot = step - 8

        @pl.loop(0, 8)
        def _(chunk):
            start = pl.multiple_of(chunk * 8, 8)
            rows = pl.ds(start, 8)
            low = pl.ds(start + NZ, 8)
            for k in range(KX):
                p, lane = k // 2, (k % 2) * NY
                re = im = None
                for t in range(8):
                    gr, gi = spec[t, k, rows, :NY], spec[t, k, rows, NY:]
                    qr = q_ref[0, t, p, rows, lane : lane + NY]
                    qi = q_ref[0, t, p, low, lane : lane + NY]
                    tr = gr * qr - gi * qi
                    ti = gr * qi + gi * qr
                    re = tr if re is None else re + tr
                    im = ti if im is None else im + ti
                work[k, rows, :NY] = re
                work[k, rows, NY:] = im

        @pl.loop(0, KX)
        def _(k):
            re, im = z_stage(tz, work[k], 1.0)
            work[k] = y_stage(jnp.concatenate([re, im], axis=1), wi_hi[...], wi_lo[...])

        scale = 1.0 / (EXT * NZ * NY)

        @pl.loop(0, 8)
        def _(chunk):
            rows = pl.ds(pl.multiple_of(chunk * 8, 8), 8)
            fr = [work[k, rows, :NY] for k in range(KX)]
            fi = [work[k, rows, NY:] for k in range(KX)]
            for m in range(5):
                even, odd = [], []
                for k in range(KX):
                    w = scale * (1.0 if k in (0, 12) else 2.0) * (-1) ** k
                    even.append((w * cos24(k * m), fr[k]))
                    odd.append((w * sin24(k * m), fi[k]))
                even = sum_terms(even)
                odd = sum_terms(odd)
                if m == 0:
                    total_ref[0, 4, rows] = even
                else:
                    if m < 4:
                        total_ref[0, 4 + m, rows] = even - odd
                    total_ref[0, 4 - m, rows] = even + odd

        shift_y = scalars[1 + 2 * slot]
        shift_z = scalars[2 + 2 * slot]
        acc = jnp.zeros((8, NY), F32)
        for x in range(8):
            e = total_ref[0, x]
            e = pltpu.roll(e, shift_y, 1)
            e = pltpu.roll(e, shift_z, 0)
            b = jnp.exp(-ENERGY_CAP * jnp.tanh(e / ENERGY_CAP))
            total_ref[0, x] = b
            for c in range(8):
                acc = acc + b[c * 8 : c * 8 + 8]
        sum_ref[0] = acc


def sum_terms(terms):
    total = None
    for coef, value in terms:
        if abs(coef) < 1e-15:
            continue
        total = coef * value if total is None else total + coef * value
    return total


def tail_kernel(
    slabs,
    probes,
    cells,
    types,
    total_ref,
    sum_ref,
    weight_ref,
    out_ref,
    mine,
    gathered,
    halo,
    mixed,
    blocks,
    part_send,
    part_recv,
    halo_send,
    halo_recv,
    block_send,
    block_recv,
):
    slots = total_ref.shape[0]
    planes = total_ref.shape[1]
    rows = out_ref.shape[1]
    slab = lax.axis_index("slab")
    probe = lax.axis_index("probe")

    barrier = pltpu.get_barrier_semaphore()

    @pl.loop(1, slabs)
    def _(d):
        pl.semaphore_signal(
            barrier, inc=1, device_id={"slab": lax.rem(slab + d, slabs)}, device_id_type=MESH
        )

    for d in range(1, probes):
        pl.semaphore_signal(
            barrier, inc=1, device_id={"probe": lax.rem(probe + d, probes)}, device_id_type=MESH
        )

    parts = []
    for s in range(slots):
        v = jnp.sum(sum_ref[s], axis=0, keepdims=True)
        v = jnp.sum(v, axis=1, keepdims=True)
        parts.append(jnp.broadcast_to(v, (1, NY)))
    parts += [jnp.zeros((1, NY), F32)] * (8 - slots)
    own = jnp.concatenate(parts, axis=0)
    mine[...] = own

    pl.semaphore_wait(barrier, slabs - 1 + probes - 1)

    def part_copy(d):
        return pltpu.make_async_remote_copy(
            src_ref=mine,
            dst_ref=gathered.at[d],
            send_sem=part_send.at[d],
            recv_sem=part_recv.at[d],
            device_id={"slab": lax.rem(slab + d, slabs)},
            device_id_type=MESH,
        )

    @pl.loop(1, slabs)
    def _(d):
        part_copy(d).start()

    to_right = pltpu.make_async_remote_copy(
        src_ref=total_ref.at[:, planes - 1],
        dst_ref=halo.at[0],
        send_sem=halo_send.at[0],
        recv_sem=halo_recv.at[0],
        device_id={"slab": lax.rem(slab + 1, slabs)},
        device_id_type=MESH,
    )
    to_left = pltpu.make_async_remote_copy(
        src_ref=total_ref.at[:, 0],
        dst_ref=halo.at[1],
        send_sem=halo_send.at[1],
        recv_sem=halo_recv.at[1],
        device_id={"slab": lax.rem(slab + slabs - 1, slabs)},
        device_id_type=MESH,
    )
    to_right.start()
    to_left.start()

    @pl.loop(1, slabs)
    def _(d):
        part_copy(d).wait_recv()

    partition = own
    for d in range(1, slabs):
        partition = partition + gathered[d]
    coef = weight_ref[...] * (cells / partition)
    coefs = [jnp.broadcast_to(coef[s : s + 1], (8, NY)) for s in range(slots)]

    def weighted(read):
        total = None
        for s in range(slots):
            v = read(s).reshape(NZ // 8, 8, NY) * coefs[s][None]
            total = v if total is None else total + v
        return total.reshape(NZ, NY)

    to_right.wait_recv()
    to_left.wait_recv()
    mixed[0] = weighted(lambda s: halo[0, s])
    mixed[planes + 1] = weighted(lambda s: halo[1, s])
    for x in range(planes):
        mixed[x + 1] = weighted(lambda s: total_ref[s, x])
    for x in range(planes):
        v = (mixed[x] + 2.0 * mixed[x + 1] + mixed[x + 2]) * 0.25
        v = (pltpu.roll(v, 1, 0) + 2.0 * v + pltpu.roll(v, NZ - 1, 0)) * 0.25
        v = (pltpu.roll(v, 1, 1) + 2.0 * v + pltpu.roll(v, NY - 1, 1)) * 0.25
        mixed[x] = v

    def block_copy(d):
        target = lax.rem(probe + d, probes)
        return pltpu.make_async_remote_copy(
            src_ref=mixed.at[pl.ds(0, planes), pl.ds(pl.multiple_of(target * rows, 8), rows)],
            dst_ref=blocks.at[d - 1],
            send_sem=block_send.at[d - 1],
            recv_sem=block_recv.at[d - 1],
            device_id={"probe": target},
            device_id_type=MESH,
        )

    for d in range(1, probes):
        block_copy(d).start()
    result = mixed[pl.ds(0, planes), pl.ds(pl.multiple_of(probe * rows, 8), rows)]
    for d in range(1, probes):
        block_copy(d).wait_recv()
        result = result + blocks[d - 1]
    out_ref[...] = result * (1.0 / types)

    @pl.loop(1, slabs)
    def _(d):
        part_copy(d).wait_send()

    to_right.wait_send()
    to_left.wait_send()
    for d in range(1, probes):
        block_copy(d).wait_send()


def rotated_cubes(library, probe_ids, rotations, core):
    slots = probe_ids.shape[0]
    perms_np, signs_np = cube_rotations()
    chosen = library[probe_ids]
    terms = chosen.shape[1]
    half = terms // 2
    chosen = jnp.where(core == 0, chosen, jnp.concatenate([chosen[:, half:], chosen[:, :half]], axis=1))
    cube = chosen.reshape(slots, terms, KS, KS, KS)
    perm = jnp.asarray(perms_np)[rotations]
    sign = jnp.asarray(signs_np)[rotations]
    zaxis = jnp.argmax(perm == 2, axis=1)
    first = jnp.where(zaxis == 0, 1, 0)
    second = jnp.where(zaxis == 2, 1, 2)
    pick = lambda table, index: jnp.take_along_axis(table, index[:, None], axis=1)[:, 0]
    layouts = [
        cube.reshape(slots, terms, KS, KS * KS),
        cube.transpose(0, 1, 3, 2, 4).reshape(slots, terms, KS, KS * KS),
        cube.transpose(0, 1, 4, 2, 3).reshape(slots, terms, KS, KS * KS),
    ]
    z4 = zaxis[:, None, None, None]
    rows = jnp.where(z4 == 0, layouts[0], jnp.where(z4 == 1, layouts[1], layouts[2]))
    sz = pick(sign, zaxis)[:, None, None, None]
    rows = jnp.where(sz > 0, rows, jnp.flip(rows, axis=2))
    flat = jnp.arange(KS * KS, dtype=jnp.int32)
    ax, ay = flat // KS - RAD, flat % KS - RAD

    def along(index):
        p, s = pick(perm, index)[:, None], pick(sign, index)[:, None]
        return s * jnp.where(p == 0, ax[None], ay[None]) + RAD

    source = along(first) * KS + along(second)
    onehot = (source[:, None, :] == flat[None, :, None]).astype(F32)
    turned = jnp.einsum(
        "srl,slm->srm", rows.reshape(slots, terms * KS, KS * KS), onehot, precision=HIGHEST
    ).reshape(slots, terms, KS, KS * KS)
    return jnp.pad(turned, ((0, 0), (0, 0), (0, AZ - KS), (0, 0)))


def local(receptor, library, probe_ids, rotations, offsets, probe_weight):
    terms, planes, nz, ny = receptor.shape
    slabs = lax.axis_size("slab")
    probes = lax.axis_size("probe")
    slots = probe_ids.shape[0]
    types = probe_weight.shape[0]
    core = lax.axis_index("probe") % 2
    half = terms // 2
    cells = float(planes * slabs * nz * ny)

    up = [(i, (i + 1) % slabs) for i in range(slabs)]
    down = [(j, i) for i, j in up]
    swap = [(i, i ^ 1) for i in range(probes)]
    share = lax.dynamic_slice_in_dim(receptor, core * half, half, axis=0)
    before_a = lax.ppermute(share, "slab", up)
    after_a = lax.ppermute(share, "slab", down)
    before_b = lax.ppermute(before_a, "probe", swap)
    after_b = lax.ppermute(after_a, "probe", swap)

    cubes = rotated_cubes(library, probe_ids, rotations[:, 0], core)
    table = jnp.asarray(xy_table().astype(np.float32))
    yk = jnp.dot(cubes.reshape(slots * terms * AZ, KS * KS), table, precision=lax.Precision.HIGH)
    yk = yk.reshape(slots * terms, AZ, PAIRS * 512)

    q = pl.pallas_call(
        probe_kernel,
        grid=(slots * terms,),
        in_specs=[
            pl.BlockSpec((128, 6 * AZ), lambda i: (0, 0)),
            pl.BlockSpec((1, AZ, PAIRS * 512), lambda i: (i, 0, 0)),
        ],
        out_specs=pl.BlockSpec((1, PAIRS, 128, 256), lambda i: (i, 0, 0, 0)),
        out_shape=jax.ShapeDtypeStruct((slots * terms, PAIRS, 128, 256), F32),
        compiler_params=pltpu.CompilerParams(vmem_limit_bytes=24 << 20),
        cost_estimate=pl.CostEstimate(
            flops=2 * slots * terms * PAIRS * 128 * 144 * 256, bytes_accessed=40 << 20, transcendentals=0
        ),
        name="probe_spectra",
    )(jnp.asarray(probe_z_table()), yk)
    q = q.reshape(slots, terms, PAIRS, 128, 256)

    scalars = jnp.concatenate([core[None].astype(jnp.int32), offsets.reshape(-1)])
    wf_hi, wf_lo = grid_y_table(-1.0)
    wi_hi, wi_lo = grid_y_table(1.0)
    plane_block = (1, planes, nz, ny)
    fixed = lambda shape: pl.BlockSpec(shape, lambda i, s: (0,) * len(shape))
    total, sums = pl.pallas_call(
        energy_kernel,
        grid_spec=pltpu.PrefetchScalarGridSpec(
            num_scalar_prefetch=1,
            grid=(terms + slots,),
            in_specs=[
                pl.BlockSpec(
                    plane_block, lambda i, s: ((jnp.minimum(i, terms - 1) + half * s[0]) % terms, 0, 0, 0)
                ),
                pl.BlockSpec(plane_block, lambda i, s: (jnp.minimum(i, half - 1), 0, 0, 0)),
                pl.BlockSpec(plane_block, lambda i, s: (jnp.clip(i - half, 0, half - 1), 0, 0, 0)),
                pl.BlockSpec(plane_block, lambda i, s: (jnp.minimum(i, half - 1), 0, 0, 0)),
                pl.BlockSpec(plane_block, lambda i, s: (jnp.clip(i - half, 0, half - 1), 0, 0, 0)),
                pl.BlockSpec(
                    (1, terms, PAIRS, 128, 256), lambda i, s: (jnp.maximum(i - terms, 0), 0, 0, 0, 0)
                ),
                fixed((128, 192)),
                fixed((256, 256)),
                fixed((256, 256)),
                fixed((256, 256)),
                fixed((256, 256)),
            ],
            out_specs=[
                pl.BlockSpec(plane_block, lambda i, s: (jnp.maximum(i - terms, 0), 0, 0, 0)),
                pl.BlockSpec((1, 8, ny), lambda i, s: (jnp.maximum(i - terms, 0), 0, 0)),
            ],
            scratch_shapes=[
                pltpu.VMEM((terms, KX, nz, 2 * ny), F32),
                pltpu.VMEM((KX, nz, 2 * ny), F32),
            ],
        ),
        out_shape=[
            jax.ShapeDtypeStruct((slots, planes, nz, ny), F32),
            jax.ShapeDtypeStruct((slots, 8, ny), F32),
        ],
        compiler_params=pltpu.CompilerParams(vmem_limit_bytes=48 << 20),
        cost_estimate=pl.CostEstimate(flops=12 << 30, bytes_accessed=40 << 20, transcendentals=1 << 20),
        name="energy_maps",
    )(
        scalars,
        receptor,
        before_a,
        before_b,
        after_a,
        after_b,
        q,
        jnp.asarray(grid_z_table()),
        jnp.asarray(wf_hi),
        jnp.asarray(wf_lo),
        jnp.asarray(wi_hi),
        jnp.asarray(wi_lo),
    )

    onehot = (probe_ids[:, None] == jnp.arange(types, dtype=jnp.int32)[None, :]).astype(F32)
    chosen = jnp.sum(onehot * probe_weight[None], axis=1)
    weight = jnp.broadcast_to(jnp.pad(chosen, (0, 8 - slots))[:, None], (8, ny))
    rows = nz // probes
    vmem = pl.BlockSpec(memory_space=pltpu.VMEM)
    return pl.pallas_call(
        functools.partial(tail_kernel, slabs, probes, cells, types),
        in_specs=[vmem] * 3,
        out_specs=vmem,
        out_shape=jax.ShapeDtypeStruct((planes, rows, ny), F32),
        scratch_shapes=[
            pltpu.VMEM((8, ny), F32),
            pltpu.VMEM((slabs, 8, ny), F32),
            pltpu.VMEM((2, slots, nz, ny), F32),
            pltpu.VMEM((planes + 2, nz, ny), F32),
            pltpu.VMEM((probes - 1, planes, rows, ny), F32),
            pltpu.SemaphoreType.DMA((slabs,)),
            pltpu.SemaphoreType.DMA((slabs,)),
            pltpu.SemaphoreType.DMA((2,)),
            pltpu.SemaphoreType.DMA((2,)),
            pltpu.SemaphoreType.DMA((probes - 1,)),
            pltpu.SemaphoreType.DMA((probes - 1,)),
        ],
        compiler_params=pltpu.CompilerParams(
            collective_id=0, has_side_effects=True, vmem_limit_bytes=24 << 20
        ),
        name="consensus_tail",
    )(total, sums, weight)


def solution(mesh):
    in_specs = (
        P(None, "slab", None, None),
        P(),
        P("probe"),
        P("probe", None),
        P("probe", None, None),
        P(),
    )
    out_specs = P("slab", "probe", None)
    return jax.shard_map(local, mesh=mesh, in_specs=in_specs, out_specs=out_specs, check_vma=False)
```

time: 698 us -> 192 us (0.28); the launches traced: 689 us -> 191 us
  matrix products: 383 us -> 12 us
  Pallas kernels: 0 us -> 110 us
  blocking collectives: 64.8 us -> 0 us
  other arithmetic: 75.9 us -> 12.1 us
  waiting for transfers between devices: 44.8 us -> 0.01 us
  between operations: 45 us -> 0.33 us
  local copies, waits for them, and re-layouts: 61.1 us -> 46.3 us
    dot_general x91 -> x2, matrix products: 383 us -> 12 us  [the longest x1 10.8 us: local(): jnp.dot(cubes.reshape(slots * terms * AZ, KS * KS), table, precision=lax....]
    pallas_call x0 -> x3, Pallas kernels: none -> 110 us  [the longest x1 70.9 us: local(): pl.pallas_call(energy_kernel, grid_spec=pltpu.PrefetchScalarGridSpec(num_...]
    psum x1 -> x0, blocking collectives: 64.8 us -> none  [local(): lax.psum(jnp.stack([jnp.sum(total) for total in totals]), 'slab')]
    reduce_scatter x1 -> x0, waiting for transfers between devices: 43.5 us -> none  [local(): lax.psum_scatter(local_smooth, 'probe', scatter_dimension=1, tiled=True)]
    select_n x8 -> x4, other arithmetic: 38.8 us -> 2.28 us  [the longest x1 2.09 us: rotated_cubes(): jnp.where(z4 == 0, layouts[0], jnp.where(z4 == 1, layouts[1], layouts[2]))]
    gather x4 -> x10, local copies, waits for them, and re-layouts: 40.4 us -> 9.61 us  [the longest x3 5.26 us: rotated_cubes(): chosen = library[probe_ids]]
    and x4 -> x0, other arithmetic: 22.6 us -> none  [rotated_kernel(): return jnp.take(library[type_id], source, axis=1)]
    reshape x4 -> x5, local copies, waits for them, and re-layouts: 2.23 us -> 23.3 us  [the longest x2 12.1 us: rotated_cubes(): cube.transpose(0, 1, 3, 2, 4).reshape(slots, terms, KS, KS * KS)]
  transfers between devices with their start and end apart: 5 -> 4, of which waited for: 2 -> 0; matrix products, arithmetic and copies ran while one was open for 50% -> 35% of each run, Pallas kernels for 0% -> 10%
where the time goes in v1:
time: 192 us; the launch traced here: 191 us
  Pallas kernels  110 us (57%)
  local copies, waits for them, and re-layouts  46.3 us (24%)
  other arithmetic  12.1 us (6%)
  matrix products  12 us (6%)
  starting transfers between devices  11 us (6%)
    pallas_call x1, Pallas kernels, local(): pl.pallas_call(energy_kernel, grid_spec=pltpu.PrefetchScalarGridSpec(num_...  70.9 us
    pallas_call x1, Pallas kernels, local(): pl.pallas_call(probe_kernel, grid=(slots * terms,), in_specs=[pl.BlockSpe...  20 us
    pallas_call x1, Pallas kernels, local(): pl.pallas_call(functools.partial(tail_kernel, slabs, probes, cells, types...  18.6 us
    reshape x2, local copies, waits for them, and re-layouts, rotated_cubes(): cube.transpose(0, 1, 3, 2, 4).reshape(slots, terms, KS, KS * KS)  12.1 us
    reshape x2, local copies, waits for them, and re-layouts, rotated_cubes(): cube.transpose(0, 1, 4, 2, 3).reshape(slots, terms, KS, KS * KS)  11.1 us
    dot_general x1, matrix products, local(): jnp.dot(cubes.reshape(slots * terms * AZ, KS * KS), table, precision=lax....  10.8 us
    transpose x1, other arithmetic, rotated_cubes(): cube.transpose(0, 1, 4, 2, 3).reshape(slots, terms, KS, KS * KS)  8.67 us
    concatenate x4, local copies, waits for them, and re-layouts, rotated_cubes(): jnp.concatenate([chosen[:, half:], chosen[:, :half]], axis=1)  8.25 us
  transfers between devices with their start and end apart: 4, of which 0 were waited for; matrix products, arithmetic and copies ran while one was open for 35% of the time, Pallas kernels for 10%

profile of v1, /device:TPU:1, one launch (start us, length us, event | category | flops | bytes accessed | tf_op | source)
XLA Modules:
  0.0 191.1 jit_solution(2698496159601877489)
XLA Ops:
  0.0 0.0 copy-start
  0.0 2.5 %constant_dynamic-slice_fusion = f32[4,8,64,128]{3,2,1,0:T(8,128)} fusion(f32[8,8,64,128]{3,2,1,0:T(8,128)} %own_ref.1, s32[]{:T(128)S(6)} %select_n.112), kind=kLoop, calls=%fused_computation.69 | loop fusion | bytes 2097156 | tf_op jit(solution)/shard_map/dynamic_slice | solution.py:488
  2.5 2.5 %collective-permute-start = (f32[4,8,64,128]{3,2,1,0:T(8,128)}, f32[4,8,64,128]{3,2,1,0:T(8,128)}, u32[]{:S(2)}, u32[]{:S(2)}) collective-permute-start(f32[4,8,64,128]{3,2,1,0:T(8,128)} %constant_dynamic-slice_fusion), channel_id=1, source_target_pairs={{0,1},{1,2},{2,3},{3,4},{4,5},{5,6},{6,7},{7,8},{8,9},{9,10},{10,1... | collective-permute-start | bytes 3145736 | tf_op jit(solution)/shard_map/ppermute | solution.py:489
  4.9 5.3 %collective-permute-start.2 = (f32[4,8,64,128]{3,2,1,0:T(8,128)}, f32[4,8,64,128]{3,2,1,0:T(8,128)}, u32[]{:S(2)}, u32[]{:S(2)}) collective-permute-start(f32[4,8,64,128]{3,2,1,0:T(8,128)} %constant_dynamic-slice_fusion), channel_id=1, source_target_pairs={{1,0},{2,1},{3,2},{4,3},{5,4},{6,5},{7,6},{8,7},{9,8},{10,9},{11,1... | collective-permute-start | bytes 3145736 | tf_op jit(solution)/shard_map/ppermute | solution.py:490
  10.3 0.0 copy-done.13
  10.3 0.0 copy-done
  10.3 0.6 gather_fusion.2
  10.9 0.1 fusion.26
  11.0 0.0 copy-start.12
  11.0 0.0 copy-start.10
  11.0 4.2 %gather.28 = f32[4,8,17,17,17]{4,3,2,1,0:T(8,128)} reshape(f32[4,8,4913]{2,1,0:T(8,128)S(1)} %gather_fusion.2) | data formatting | bytes 1257728 | tf_op jit(solution)/shard_map/gather | solution.py:440
  15.2 0.6 gather_fusion
  15.8 0.7 iota_reduce_fusion
  16.5 3.0 %concatenate.22 = f32[4,4,17,17,17]{4,3,2,1,0:T(8,128)} reshape(f32[4,4,4913]{2,1,0:T(4,128)S(1)} %get-tuple-element.14) | data formatting | bytes 628864 | tf_op jit(solution)/shard_map/concatenate | solution.py:443
  19.5 1.1 concatenate.19
  20.6 3.0 %concatenate.23 = f32[4,4,17,17,17]{4,3,2,1,0:T(8,128)} reshape(f32[4,4,4913]{2,1,0:T(4,128)S(1)} %get-tuple-element.15) | data formatting | bytes 628864 | tf_op jit(solution)/shard_map/concatenate | solution.py:443
  23.6 1.1 concatenate.20
  24.8 0.5 gather.27
  25.2 0.6 gather_fusion.1
  25.8 0.6 gather_fusion.7
  26.5 0.6 gather_fusion.5
  27.1 0.6 gather_fusion.6
  27.8 0.6 gather_fusion.4
  28.4 8.7 %fusion.1 = (f32[4,8,17,17,17]{2,4,3,1,0:T(8,128)}, f32[4,8,17,17,17]{4,2,3,1,0:T(8,128)}) fusion(f32[4,8,17,17,17]{4,3,2,1,0:T(8,128)} %gather.28, f32[4,4,17,17,17]{4,3,2,1,0:T(8,128)} %concatenate.23, f32[4,4,17,17,17]{4,3,2,1,0:T(8,128)} %concatenate.22, pred[]{:T(512)S(6)} %eq.58), kind=kLoop, calls=%fused_computation.11 | loop fusion | flops 314432 | bytes 2515457 | tf_op jit(solution)/shard_map/transpose | solution.py:454
  37.1 6.7 %copy.36 = f32[4,8,17,17,17]{4,3,2,1,0:T(8,128)} copy(f32[4,8,17,17,17]{4,2,3,1,0:T(8,128)} %get-tuple-element.13) | data formatting | bytes 1257728 | tf_op jit(solution)/shard_map/reshape | solution.py:453
  43.8 5.4 %reshape.299 = f32[4,8,17,289]{3,2,1,0:T(8,128)} reshape(f32[4,8,17,17,17]{4,3,2,1,0:T(8,128)} %copy.36) | data formatting | bytes 1257728 | tf_op jit(solution)/shard_map/reshape | solution.py:453
  49.2 6.7 %reshape.300 = f32[4,8,17,289]{2,3,1,0:T(8,128)} reshape(f32[4,8,17,17,17]{2,4,3,1,0:T(8,128)} %get-tuple-element.12) | data formatting | bytes 1257728 | tf_op jit(solution)/shard_map/reshape | solution.py:454
  55.9 4.4 %copy.31 = f32[4,8,17,289]{3,2,1,0:T(8,128)} copy(f32[4,8,17,289]{2,3,1,0:T(8,128)} %reshape.300) | data formatting | bytes 1257728 | tf_op jit(solution)/shard_map/reshape | solution.py:454
  60.3 0.6 gather_fusion.3
  61.0 2.1 %fusion.3 = f32[4,8,17,289]{3,2,1,0:T(8,128)S(1)} fusion(f32[4,8,17,289]{3,2,1,0:T(8,128)S(1)} %gather.27, f32[4,4,17,289]{3,2,1,0:T(8,128)} %concatenate.20, f32[4,4,17,289]{3,2,1,0:T(8,128)S(1)} %copy-done.8, f32[4,8,17,289]{3,2,1,0:T(8,128)} %reshape.299, f32[4,8,17,289]{3,2,1,0:T(8,128)} %copy.31, pred[4]{0:T(512)(128)(4,1)S(1)} %get-tuple-element.18, ...), kind=kLoop, calls=%fused_computation.14 | loop fusion | flops 628864 | bytes 3144329 | tf_op jit(solution)/shard_map/jit(_where)/select_n | solution.py:457
  63.1 0.5 rev.4
  63.5 0.2 broadcast_select_fusion
  63.7 0.5 copy.32
  64.3 0.1 add_add_fusion
  64.4 1.2 fusion
  65.6 0.0 copy-start.11
  65.6 0.2 copy.34
  65.9 0.0 copy-start.14
  65.9 0.1 copy.40
  66.0 0.3 copy-done.11
  66.3 0.1 copy.27
  66.4 0.1 reshape.198
  66.5 0.1 pad.8.clone
  66.6 0.0 collective-permute-done.before_a
  66.6 3.1 %collective-permute-start.1 = (f32[4,8,64,128]{3,2,1,0:T(8,128)}, f32[4,8,64,128]{3,2,1,0:T(8,128)S(1)}, u32[]{:S(2)}, u32[]{:S(2)}) collective-permute-start(f32[4,8,64,128]{3,2,1,0:T(8,128)} %collective-permute-done.before_a), channel_id=1, source_target_pairs={{0,32},{32,0},{64,96},{96,64},{1,33},{33,1},{65,97},{97,65},{2,34}... | collective-permute-start | bytes 3145736 | tf_op jit(solution)/shard_map/ppermute | solution.py:491
  69.6 0.0 collective-permute-done.2.after_a
  69.6 0.1 collective-permute-start.3
  69.7 0.2 select_reduce_fusion
  69.9 0.1 pad_add_fusion.3.scalars
  70.0 10.8 %fusion.27.y_ref = f32[32,24,3584]{2,1,0:T(8,128)S(1)} fusion(f32[32,24,289]{2,1,0:T(8,128)S(1)} %bitcast.89, f32[289,3584,1]{1,0,2:T(8,128)} %constant.205), kind=kOutput, calls=%fused_computation.74 | convolution fusion | flops 4772855808 | bytes 16040960 | tf_op jit(solution)/shard_map/dot_general | solution.py:496
  80.8 0.0 copy-start.3
  80.8 0.0 copy-start.4
  80.8 0.0 copy-start.5
  80.8 0.0 copy-start.6
  80.8 0.0 copy-start.7
  80.8 20.0 %probe_spectra.1 = f32[32,7,128,256]{3,2,1,0:T(8,128)} custom-call(bf16[128,144]{1,0:T(8,128)(2,1)S(1)} %copy-done.2, f32[32,24,3584]{2,1,0:T(8,128)S(1)} %fusion.27.y_ref), custom_call_target="tpu_custom_call" | custom-call | flops 2113929216 | bytes 41943040 | tf_op jit(solution)/shard_map/probe_spectra/pallas_call | solution.py:499
  100.8 0.0 collective-permute-done.1.before_b
  100.8 0.0 collective-permute-done.3.after_b
  100.9 0.0 copy-start.1
  100.9 70.9 %energy_maps.1 = (f32[4,8,64,128]{3,2,1,0:T(8,128)S(1)}, f32[4,8,128]{2,1,0:T(8,128)S(1)}) custom-call(s32[9]{0:T(128)S(1)} %pad_add_fusion.3.scalars, f32[8,8,64,128]{3,2,1,0:T(8,128)} %own_ref.1, f32[4,8,64,128]{3,2,1,0:T(8,128)} %collective-permute-done.before_a, f32[4,8,64,128]{3,2,1,0:T(8,128)S(1)} %collective-permute-done.1.before_b, ...), custom_call_target="tpu_custom_call" | custom-call | flops 12884901888 | bytes 41943040 | tf_op jit(solution)/shard_map/energy_maps/pallas_call | solution.py:521
  171.8 0.1 broadcast_in_dim.113.weight_ref
  171.9 18.6 %consensus_tail.1 = f32[8,16,128]{2,1,0:T(8,128)S(1)} custom-call(f32[4,8,64,128]{3,2,1,0:T(8,128)S(1)} %get-tuple-element.10.total_ref, f32[4,8,128]{2,1,0:T(8,128)S(1)} %get-tuple-element.11.sum_ref, f32[8,128]{1,0:T(8,128)S(1)} %broadcast_in_dim.113.weight_ref), custom_call_target="tpu_custom_call" | custom-call | tf_op jit(solution)/shard_map/consensus_tail/pallas_call | solution.py:579
  190.5 0.6 copy.44
  191.1 0.0 copy-done.1
  (30 shorter events, 0.1 us)
Async XLA Ops:
  0.0 10.3 %copy-start = (f32[16,8,4913]{2,1,0:T(8,128)S(1)}, f32[16,8,4913]{2,1,0:T(8,128)}, u32[]{:S(2)}) copy-start(f32[16,8,4913]{2,1,0:T(8,128)} %param.18) | copy-start | bytes 7546372
  0.0 10.3 %copy-start.13 = (s32[4]{0:T(128)S(1)}, s32[4]{0:T(128)}, u32[]{:S(2)}) copy-start(s32[4]{0:T(128)} %param.19) | copy-start | bytes 52
  2.5 64.1 %collective-permute-start = (f32[4,8,64,128]{3,2,1,0:T(8,128)}, f32[4,8,64,128]{3,2,1,0:T(8,128)}, u32[]{:S(2)}, u32[]{:S(2)}) collective-permute-start(f32[4,8,64,128]{3,2,1,0:T(8,128)} %constant_dynamic-slice_fusion), channel_id=1, source_target_pairs={{0,1},{1,2},{2,3},{3,4},{4,5},{5,6},{6,7},{7,8},{8,9},{9,10},{10,1... | collective-permute-start | bytes 3145736 | tf_op jit(solution)/shard_map/ppermute | solution.py:489
  4.9 64.7 %collective-permute-start.2 = (f32[4,8,64,128]{3,2,1,0:T(8,128)}, f32[4,8,64,128]{3,2,1,0:T(8,128)}, u32[]{:S(2)}, u32[]{:S(2)}) collective-permute-start(f32[4,8,64,128]{3,2,1,0:T(8,128)} %constant_dynamic-slice_fusion), channel_id=1, source_target_pairs={{1,0},{2,1},{3,2},{4,3},{5,4},{6,5},{7,6},{8,7},{9,8},{10,9},{11,1... | collective-permute-start | bytes 3145736 | tf_op jit(solution)/shard_map/ppermute | solution.py:490
  11.0 4.2 %copy-start.12 = (s32[4,1]{0,1:T(1,128)S(1)}, s32[4,1]{0,1:T(1,128)}, u32[]{:S(2)}) copy-start(s32[4,1]{0,1:T(1,128)} %param.20) | copy-start | bytes 52
  11.0 4.2 %copy-start.10 = (s32[24,3]{1,0:T(8,128)S(1)}, s32[24,3]{1,0:T(8,128)}, u32[]{:S(2)}) copy-start(s32[24,3]{1,0:T(8,128)} %constant.110.clone) | copy-start | bytes 868
  23.6 1.6 copy-start.9
  55.9 5.1 %copy-start.8 = (f32[4,4,17,289]{3,2,1,0:T(8,128)S(1)}, f32[4,4,17,289]{3,2,1,0:T(8,128)}, u32[]{:S(2)}) copy-start(f32[4,4,17,289]{3,2,1,0:T(8,128)} %concatenate.19) | copy-start | bytes 943300
  65.6 0.7 copy-start.11
  65.9 3.9 %copy-start.14 = (f32[16]{0:T(128)S(1)}, f32[16]{0:T(128)}, u32[]{:S(2)}) copy-start(f32[16]{0:T(128)} %param.22) | copy-start | bytes 196
  66.6 34.2 %collective-permute-start.1 = (f32[4,8,64,128]{3,2,1,0:T(8,128)}, f32[4,8,64,128]{3,2,1,0:T(8,128)S(1)}, u32[]{:S(2)}, u32[]{:S(2)}) collective-permute-start(f32[4,8,64,128]{3,2,1,0:T(8,128)} %collective-permute-done.before_a), channel_id=1, source_target_pairs={{0,32},{32,0},{64,96},{96,64},{1,33},{33,1},{65,97},{97,65},{2,34}... | collective-permute-start | bytes 3145736 | tf_op jit(solution)/shard_map/ppermute | solution.py:491
  69.6 31.2 %collective-permute-start.3 = (f32[4,8,64,128]{3,2,1,0:T(8,128)}, f32[4,8,64,128]{3,2,1,0:T(8,128)S(1)}, u32[]{:S(2)}, u32[]{:S(2)}) collective-permute-start(f32[4,8,64,128]{3,2,1,0:T(8,128)} %collective-permute-done.2.after_a), channel_id=1, source_target_pairs={{0,32},{32,0},{64,96},{96,64},{1,33},{33,1},{65,97},{97,65},{2,34}... | collective-permute-start | bytes 3145736 | tf_op jit(solution)/shard_map/ppermute | solution.py:492
  70.0 10.8 %copy-start.2 = (bf16[128,144]{1,0:T(8,128)(2,1)S(1)}, bf16[128,144]{1,0:T(8,128)(2,1)}, u32[]{:S(2)}) copy-start(bf16[128,144]{1,0:T(8,128)(2,1)} %constant.113.clone.tz_ref) | copy-start | bytes 110596
  80.8 20.0 %copy-start.3 = (bf16[256,256]{1,0:T(8,128)(2,1)S(1)}, bf16[256,256]{1,0:T(8,128)(2,1)}, u32[]{:S(2)}) copy-start(bf16[256,256]{1,0:T(8,128)(2,1)} %constant.115.clone.wf_hi) | copy-start | bytes 393220
  80.8 20.0 %copy-start.4 = (bf16[256,256]{1,0:T(8,128)(2,1)S(1)}, bf16[256,256]{1,0:T(8,128)(2,1)}, u32[]{:S(2)}) copy-start(bf16[256,256]{1,0:T(8,128)(2,1)} %constant.116.clone.wf_lo) | copy-start | bytes 393220
  80.8 20.0 %copy-start.5 = (bf16[256,256]{1,0:T(8,128)(2,1)S(1)}, bf16[256,256]{1,0:T(8,128)(2,1)}, u32[]{:S(2)}) copy-start(bf16[256,256]{1,0:T(8,128)(2,1)} %constant.117.clone.wi_hi) | copy-start | bytes 393220
  80.8 20.0 %copy-start.6 = (bf16[256,256]{1,0:T(8,128)(2,1)S(1)}, bf16[256,256]{1,0:T(8,128)(2,1)}, u32[]{:S(2)}) copy-start(bf16[256,256]{1,0:T(8,128)(2,1)} %constant.118.clone.wi_lo) | copy-start | bytes 393220
  80.8 20.0 %copy-start.7 = (bf16[128,192]{1,0:T(8,128)(2,1)S(1)}, bf16[128,192]{1,0:T(8,128)(2,1)}, u32[]{:S(2)}) copy-start(bf16[128,192]{1,0:T(8,128)(2,1)} %constant.114.clone.tz_ref) | copy-start | bytes 147460
  100.9 90.3 %copy-start.1 = (f32[16,8,4913]{2,1,0:T(8,128)S(1)}, f32[16,8,4913]{2,1,0:T(8,128)}, u32[]{:S(2)}) copy-start(f32[16,8,4913]{2,1,0:T(8,128)} %param.18) | copy-start | bytes 7546372

commit v2 on v1

--- a/solution.py
+++ b/solution.py
@@ -46,17 +46,62 @@
     return hi, lo
 
 
-def xy_table():
-    a = np.arange(KS) - RAD
+HALF = (KS * KS + 1) // 2
+CUBE = 384
+PACK = 512
+
+
+def half_offsets():
+    flat = np.arange(HALF) + HALF - 1
+    return flat // KS - RAD, flat % KS - RAD
+
+
+def xy_tables():
+    ax, ay = half_offsets()
     kx = np.arange(2 * PAIRS)
     ky = np.arange(NY)
-    px = (a[:, None] * kx[None, :]) % EXT / EXT
-    py = (a[:, None] * ky[None, :]) % NY / NY
-    ang = 2 * np.pi * (px[:, None, :, None] + py[None, :, None, :])
-    live = (kx < KX).astype(np.float64)[None, None, :, None]
-    both = np.stack([np.cos(ang) * live, np.sin(ang) * live], axis=2)
-    both = both.reshape(KS, KS, 2, PAIRS, 2, NY).transpose(0, 1, 3, 2, 4, 5)
-    return both.reshape(KS * KS, PAIRS * 2 * 2 * NY)
+    px = (ax[:, None] * kx[None, :]) % EXT / EXT
+    py = (ay[:, None] * ky[None, :]) % NY / NY
+    ang = 2 * np.pi * (px[:, :, None] + py[:, None, :])
+    live = (kx < KX).astype(np.float64)[None, :, None]
+    out = []
+    for t in (np.cos(ang) * live, np.sin(ang) * live):
+        hi, lo = split_np(t.reshape(HALF, -1))
+        pad = np.zeros((PACK - 3 * HALF, hi.shape[1]), hi.dtype)
+        out.append(np.concatenate([hi, hi, lo, pad], axis=0))
+    return out
+
+
+def lane_offsets():
+    ax, ay = half_offsets()
+    rows = np.full((8, PACK), 10000, np.int32)
+    for c in range(3):
+        rows[0, c * HALF : (c + 1) * HALF] = ax
+        rows[1, c * HALF : (c + 1) * HALF] = ay
+    rows[2] = 0
+    rows[2, [0, HALF, 2 * HALF]] = 10000
+    return rows
+
+
+def swap_table():
+    t = np.zeros((CUBE, CUBE), np.float32)
+    for m in range(KS):
+        for n in range(KS):
+            t[n * KS + m, m * KS + n] = 1
+    return t.astype(ml_dtypes.bfloat16)
+
+
+def rotation_table():
+    perms, signs = cube_rotations()
+    table = np.zeros((24, 4), np.int32)
+    for q in range(24):
+        zaxis = [i for i in range(3) if perms[q, i] == 2][0]
+        others = [i for i in range(3) if i != zaxis]
+        table[q, 0] = zaxis
+        table[q, 1] = 1 if signs[q, zaxis] < 0 else 0
+        for i, unit in zip(others, (KS, 1)):
+            table[q, 2 + perms[q, i]] = unit * signs[q, i]
+    return table
 
 
 def probe_z_table():
@@ -82,7 +127,8 @@
     k = np.arange(NY)
     ang = 2 * np.pi * ((k[:, None] * k[None, :]) % NY) / NY
     c, s = np.cos(ang), direction * np.sin(ang)
-    return split_np(np.block([[c, s], [-s, c]]))
+    hi, lo = split_np(np.block([[c, s], [-s, c]]))
+    return np.concatenate([hi, hi, lo], axis=0)
 
 
 def split(x):
@@ -91,15 +137,127 @@
     return hi, lo
 
 
-def probe_kernel(tz_ref, y_ref, q_ref):
+def probe_kernel(
+    ids, rots, core, turns, lib_ref, swap_ref, lane_ref, te_ref, to_ref, tz_ref, q_ref, xa, xb, kd, even, odd
+):
+    slots = ids.shape[0]
+    terms = lib_ref.shape[1]
+
+    @pl.when(pl.program_id(0) == 0)
+    def _():
+        xa[...] = jnp.zeros_like(xa)
+        kd[...] = jnp.zeros_like(kd)
+        lane = lax.broadcasted_iota(jnp.int32, (terms, CUBE), 1)
+        packed_lane = lax.broadcasted_iota(jnp.int32, (terms * AZ, 128), 1)
+        source = lax.broadcasted_iota(jnp.int32, (CUBE, PACK), 0)
+
+        @pl.loop(0, slots)
+        def _(slot):
+            rot = rots[slot]
+            zaxis, flipped = turns[rot, 0], turns[rot, 1]
+            step_x, step_y = turns[rot, 2], turns[rot, 3]
+            for m in range(KS):
+                w = lib_ref[ids[slot], :, m * KS * KS : (m + 1) * KS * KS]
+                xa[m, :, : KS * KS] = pltpu.roll(w, core[0] * (terms // 2), 0)
+
+            def permuted(x, table):
+                hi, lo = split(x)
+                out = jnp.dot(jnp.concatenate([hi, lo], axis=0), table, preferred_element_type=F32)
+                return out[: x.shape[0]] + out[x.shape[0] :]
+
+            @pl.when(zaxis == 2)
+            def _():
+                turned = permuted(xa[...].reshape(KS * terms, CUBE), swap_ref[...])
+                xa[...] = turned.reshape(KS, terms, CUBE)
+
+            @pl.when(zaxis == 0)
+            def _():
+                xb[...] = xa[...]
+
+            @pl.when(zaxis > 0)
+            def _():
+                for m in range(KS):
+                    acc = jnp.zeros((terms, CUBE), F32)
+                    for n in range(KS):
+                        moved = pltpu.roll(xa[n], ((n - m) * KS) % CUBE, 1)
+                        acc = jnp.where((lane >= n * KS) & (lane < (n + 1) * KS), moved, acc)
+                    xb[m] = acc
+
+            here = lane_ref[0:1] * step_x + lane_ref[1:2] * step_y + (HALF - 1)
+            there = 2 * (HALF - 1) - here + lane_ref[2:3]
+            plus = (source == here).astype(F32)
+            minus = (source == there).astype(F32)
+            x = xb[...].reshape(KS * terms, CUBE)
+            for table, ref in ((plus + minus, even), (plus - minus, odd)):
+                turned = permuted(x, table.astype(BF))
+                for m in range(KS):
+                    az = jnp.where(flipped == 1, KS - 1 - m, m)
+                    for j in range(PACK // 128):
+                        kd[j, pl.ds(az, terms, stride=AZ), :] = turned[
+                            m * terms : (m + 1) * terms, j * 128 : (j + 1) * 128
+                        ]
+                rows = pl.ds(pl.multiple_of(slot * terms * AZ, terms * AZ), terms * AZ)
+                for j in range(PACK // 128):
+                    hi, lo = split(kd[j])
+                    packed = packed_lane + j * 128
+                    low = (packed >= HALF) & (packed < 2 * HALF)
+                    ref[rows, j * 128 : (j + 1) * 128] = jnp.where(
+                        low, lo.astype(F32), hi.astype(F32)
+                    ).astype(BF)
+
     tz = tz_ref[...]
-    for p in range(PAIRS):
-        d = jnp.concatenate(
-            [y_ref[0, :, p * 512 : p * 512 + 256], y_ref[0, :, p * 512 + 256 : p * 512 + 512]], axis=0
-        )
+    re = jnp.dot(even[...], te_ref[...], preferred_element_type=F32)
+    im = jnp.dot(odd[...], to_ref[...], preferred_element_type=F32)
+    for i in range(slots * terms):
+        d = jnp.concatenate([re[i * AZ : (i + 1) * AZ], im[i * AZ : (i + 1) * AZ]], axis=0)
         hi, lo = split(d)
-        rhs = jnp.concatenate([hi, hi, lo], axis=0)
-        q_ref[0, p] = jnp.dot(tz, rhs, preferred_element_type=F32)
+        q_ref[i, 0] = jnp.dot(tz, jnp.concatenate([hi, hi, lo], axis=0), preferred_element_type=F32)
+
+
+def probe_call(library, probe_ids, rotations, core):
+    slots, terms = probe_ids.shape[0], library.shape[1]
+    te, to = xy_tables()
+    fixed = lambda shape: pl.BlockSpec(shape, lambda i, *s: (0,) * len(shape))
+    table = pl.BlockSpec((PACK, 256), lambda i, *s: (0, i))
+    q = pl.pallas_call(
+        probe_kernel,
+        grid_spec=pltpu.PrefetchScalarGridSpec(
+            num_scalar_prefetch=4,
+            grid=(PAIRS,),
+            in_specs=[
+                fixed(library.shape),
+                fixed((CUBE, CUBE)),
+                fixed((8, PACK)),
+                table,
+                table,
+                fixed((128, 6 * AZ)),
+            ],
+            out_specs=pl.BlockSpec((slots * terms, 1, 128, 256), lambda i, *s: (0, i, 0, 0)),
+            scratch_shapes=[
+                pltpu.VMEM((KS, terms, CUBE), F32),
+                pltpu.VMEM((KS, terms, CUBE), F32),
+                pltpu.VMEM((PACK // 128, terms * AZ, 128), F32),
+                pltpu.VMEM((slots * terms * AZ, PACK), BF),
+                pltpu.VMEM((slots * terms * AZ, PACK), BF),
+            ],
+        ),
+        out_shape=jax.ShapeDtypeStruct((slots * terms, PAIRS, 128, 256), F32),
+        compiler_params=pltpu.CompilerParams(vmem_limit_bytes=40 << 20),
+        cost_estimate=pl.CostEstimate(flops=8 << 30, bytes_accessed=40 << 20, transcendentals=0),
+        name="probe_spectra",
+    )(
+        probe_ids,
+        rotations,
+        core,
+        jnp.asarray(rotation_table()),
+        library,
+        jnp.asarray(swap_table()),
+        jnp.asarray(lane_offsets()),
+        jnp.asarray(te),
+        jnp.asarray(to),
+        jnp.asarray(probe_z_table()),
+    )
+    return q.reshape(slots, terms, PAIRS, 128, 256)
 
 
 def cos24(m):
@@ -153,11 +311,9 @@
     return re, im
 
 
-def y_stage(x, w_hi, w_lo):
+def y_stage(x, w):
     hi, lo = split(x)
-    out = jnp.dot(hi, w_hi, preferred_element_type=F32)
-    out = out + jnp.dot(lo, w_hi, preferred_element_type=F32)
-    return out + jnp.dot(hi, w_lo, preferred_element_type=F32)
+    return jnp.dot(jnp.concatenate([hi, lo, hi], axis=1), w, preferred_element_type=F32)
 
 
 def z_stage(tz, x, direction):
@@ -178,10 +334,8 @@
     after_b,
     q_ref,
     tz_ref,
-    wf_hi,
-    wf_lo,
-    wi_hi,
-    wi_lo,
+    wf_ref,
+    wi_ref,
     total_ref,
     sum_ref,
     spec,
@@ -204,10 +358,10 @@
                 work[k, rows, :NY] = re[k]
                 work[k, rows, NY:] = im[k] if im[k] is not None else jnp.zeros_like(re[k])
 
-        @pl.loop(0, KX)
-        def _(k):
-            y = y_stage(work[k], wf_hi[...], wf_lo[...])
-            re, im = z_stage(tz, y, -1.0)
+        y = y_stage(work[...].reshape(KX * NZ, 2 * NY), wf_ref[...])
+        work[...] = y.reshape(KX, NZ, 2 * NY)
+        for k in range(KX):
+            re, im = z_stage(tz, work[k], -1.0)
             spec[step, k, :, :NY] = re
             spec[step, k, :, NY:] = im
 
@@ -242,10 +396,12 @@
                 work[k, rows, :NY] = re
                 work[k, rows, NY:] = im
 
-        @pl.loop(0, KX)
-        def _(k):
+        for k in range(KX):
             re, im = z_stage(tz, work[k], 1.0)
-            work[k] = y_stage(jnp.concatenate([re, im], axis=1), wi_hi[...], wi_lo[...])
+            work[k, :, :NY] = re
+            work[k, :, NY:] = im
+        y = y_stage(work[...].reshape(KX * NZ, 2 * NY), wi_ref[...])
+        work[...] = y.reshape(KX, NZ, 2 * NY)
 
         scale = 1.0 / (EXT * NZ * NY)
 
@@ -434,91 +590,12 @@
         block_copy(d).wait_send()
 
 
-def rotated_cubes(library, probe_ids, rotations, core):
-    slots = probe_ids.shape[0]
-    perms_np, signs_np = cube_rotations()
-    chosen = library[probe_ids]
-    terms = chosen.shape[1]
-    half = terms // 2
-    chosen = jnp.where(core == 0, chosen, jnp.concatenate([chosen[:, half:], chosen[:, :half]], axis=1))
-    cube = chosen.reshape(slots, terms, KS, KS, KS)
-    perm = jnp.asarray(perms_np)[rotations]
-    sign = jnp.asarray(signs_np)[rotations]
-    zaxis = jnp.argmax(perm == 2, axis=1)
-    first = jnp.where(zaxis == 0, 1, 0)
-    second = jnp.where(zaxis == 2, 1, 2)
-    pick = lambda table, index: jnp.take_along_axis(table, index[:, None], axis=1)[:, 0]
-    layouts = [
-        cube.reshape(slots, terms, KS, KS * KS),
-        cube.transpose(0, 1, 3, 2, 4).reshape(slots, terms, KS, KS * KS),
-        cube.transpose(0, 1, 4, 2, 3).reshape(slots, terms, KS, KS * KS),
-    ]
-    z4 = zaxis[:, None, None, None]
-    rows = jnp.where(z4 == 0, layouts[0], jnp.where(z4 == 1, layouts[1], layouts[2]))
-    sz = pick(sign, zaxis)[:, None, None, None]
-    rows = jnp.where(sz > 0, rows, jnp.flip(rows, axis=2))
-    flat = jnp.arange(KS * KS, dtype=jnp.int32)
-    ax, ay = flat // KS - RAD, flat % KS - RAD
-
-    def along(index):
-        p, s = pick(perm, index)[:, None], pick(sign, index)[:, None]
-        return s * jnp.where(p == 0, ax[None], ay[None]) + RAD
-
-    source = along(first) * KS + along(second)
-    onehot = (source[:, None, :] == flat[None, :, None]).astype(F32)
-    turned = jnp.einsum(
-        "srl,slm->srm", rows.reshape(slots, terms * KS, KS * KS), onehot, precision=HIGHEST
-    ).reshape(slots, terms, KS, KS * KS)
-    return jnp.pad(turned, ((0, 0), (0, 0), (0, AZ - KS), (0, 0)))
-
-
-def local(receptor, library, probe_ids, rotations, offsets, probe_weight):
+def energy_call(scalars, receptor, before_a, before_b, after_a, after_b, q):
     terms, planes, nz, ny = receptor.shape
-    slabs = lax.axis_size("slab")
-    probes = lax.axis_size("probe")
-    slots = probe_ids.shape[0]
-    types = probe_weight.shape[0]
-    core = lax.axis_index("probe") % 2
-    half = terms // 2
-    cells = float(planes * slabs * nz * ny)
-
-    up = [(i, (i + 1) % slabs) for i in range(slabs)]
-    down = [(j, i) for i, j in up]
-    swap = [(i, i ^ 1) for i in range(probes)]
-    share = lax.dynamic_slice_in_dim(receptor, core * half, half, axis=0)
-    before_a = lax.ppermute(share, "slab", up)
-    after_a = lax.ppermute(share, "slab", down)
-    before_b = lax.ppermute(before_a, "probe", swap)
-    after_b = lax.ppermute(after_a, "probe", swap)
-
-    cubes = rotated_cubes(library, probe_ids, rotations[:, 0], core)
-    table = jnp.asarray(xy_table().astype(np.float32))
-    yk = jnp.dot(cubes.reshape(slots * terms * AZ, KS * KS), table, precision=lax.Precision.HIGH)
-    yk = yk.reshape(slots * terms, AZ, PAIRS * 512)
-
-    q = pl.pallas_call(
-        probe_kernel,
-        grid=(slots * terms,),
-        in_specs=[
-            pl.BlockSpec((128, 6 * AZ), lambda i: (0, 0)),
-            pl.BlockSpec((1, AZ, PAIRS * 512), lambda i: (i, 0, 0)),
-        ],
-        out_specs=pl.BlockSpec((1, PAIRS, 128, 256), lambda i: (i, 0, 0, 0)),
-        out_shape=jax.ShapeDtypeStruct((slots * terms, PAIRS, 128, 256), F32),
-        compiler_params=pltpu.CompilerParams(vmem_limit_bytes=24 << 20),
-        cost_estimate=pl.CostEstimate(
-            flops=2 * slots * terms * PAIRS * 128 * 144 * 256, bytes_accessed=40 << 20, transcendentals=0
-        ),
-        name="probe_spectra",
-    )(jnp.asarray(probe_z_table()), yk)
-    q = q.reshape(slots, terms, PAIRS, 128, 256)
-
-    scalars = jnp.concatenate([core[None].astype(jnp.int32), offsets.reshape(-1)])
-    wf_hi, wf_lo = grid_y_table(-1.0)
-    wi_hi, wi_lo = grid_y_table(1.0)
+    slots, half = q.shape[0], terms // 2
     plane_block = (1, planes, nz, ny)
     fixed = lambda shape: pl.BlockSpec(shape, lambda i, s: (0,) * len(shape))
-    total, sums = pl.pallas_call(
+    return pl.pallas_call(
         energy_kernel,
         grid_spec=pltpu.PrefetchScalarGridSpec(
             num_scalar_prefetch=1,
@@ -535,10 +612,8 @@
                     (1, terms, PAIRS, 128, 256), lambda i, s: (jnp.maximum(i - terms, 0), 0, 0, 0, 0)
                 ),
                 fixed((128, 192)),
-                fixed((256, 256)),
-                fixed((256, 256)),
-                fixed((256, 256)),
-                fixed((256, 256)),
+                fixed((768, 256)),
+                fixed((768, 256)),
             ],
             out_specs=[
                 pl.BlockSpec(plane_block, lambda i, s: (jnp.maximum(i - terms, 0), 0, 0, 0)),
@@ -565,11 +640,34 @@
         after_b,
         q,
         jnp.asarray(grid_z_table()),
-        jnp.asarray(wf_hi),
-        jnp.asarray(wf_lo),
-        jnp.asarray(wi_hi),
-        jnp.asarray(wi_lo),
+        jnp.asarray(grid_y_table(-1.0)),
+        jnp.asarray(grid_y_table(1.0)),
     )
+
+
+def local(receptor, library, probe_ids, rotations, offsets, probe_weight):
+    terms, planes, nz, ny = receptor.shape
+    slabs = lax.axis_size("slab")
+    probes = lax.axis_size("probe")
+    slots = probe_ids.shape[0]
+    types = probe_weight.shape[0]
+    core = lax.axis_index("probe") % 2
+    half = terms // 2
+    cells = float(planes * slabs * nz * ny)
+
+    up = [(i, (i + 1) % slabs) for i in range(slabs)]
+    down = [(j, i) for i, j in up]
+    swap = [(i, i ^ 1) for i in range(probes)]
+    share = lax.dynamic_slice_in_dim(receptor, core * half, half, axis=0)
+    before_a = lax.ppermute(share, "slab", up)
+    after_a = lax.ppermute(share, "slab", down)
+    before_b = lax.ppermute(before_a, "probe", swap)
+    after_b = lax.ppermute(after_a, "probe", swap)
+
+    q = probe_call(library, probe_ids, rotations[:, 0], core[None].astype(jnp.int32))
+
+    scalars = jnp.concatenate([core[None].astype(jnp.int32), offsets.reshape(-1)])
+    total, sums = energy_call(scalars, receptor, before_a, before_b, after_a, after_b, q)
 
     onehot = (probe_ids[:, None] == jnp.arange(types, dtype=jnp.int32)[None, :]).astype(F32)
     chosen = jnp.sum(onehot * probe_weight[None], axis=1)

time: 192 us -> 106 us (0.55)
  Pallas kernels: 110 us -> 65.8 us
  local copies, waits for them, and re-layouts: 46.3 us -> 7.12 us
  waiting for transfers between devices: 0.01 us -> 22.8 us
  matrix products: 12 us -> 0 us
  other arithmetic: 12.1 us -> 0.93 us
    pallas_call x2, Pallas kernels: 90.9 us -> 45.8 us  [the longest x1 26.5 us: energy_call(): pl.pallas_call(energy_kernel, grid_spec=pltpu.PrefetchScalarGridSpec(num_...]
    reshape x4 -> x0, local copies, waits for them, and re-layouts: 23.2 us -> none  [the longest x2 12.1 us: rotated_cubes(): cube.transpose(0, 1, 3, 2, 4).reshape(slots, terms, KS, KS * KS)]
    ppermute x1, waiting for transfers between devices: 0.01 us -> 22.8 us  [local(): before_a = lax.ppermute(share, 'slab', up)]
    dot_general x2 -> x0, matrix products: 12 us -> none  [the longest x1 10.8 us: local(): jnp.dot(cubes.reshape(slots * terms * AZ, KS * KS), table, precision=lax....]
    gather x10 -> x0, local copies, waits for them, and re-layouts: 9.61 us -> none  [the longest x3 5.26 us: rotated_cubes(): chosen = library[probe_ids]]
    transpose x1 -> x0, other arithmetic: 8.67 us -> none  [rotated_cubes(): cube.transpose(0, 1, 4, 2, 3).reshape(slots, terms, KS, KS * KS)]
    concatenate x4 -> x0, local copies, waits for them, and re-layouts: 8.25 us -> none  [rotated_cubes(): jnp.concatenate([chosen[:, half:], chosen[:, :half]], axis=1)]
    unnamed x34 -> x26, local copies, waits for them, and re-layouts: 1.24 us -> 5.49 us
  transfers between devices with their start and end apart: 4 -> 4, of which waited for: 0 -> 1; matrix products, arithmetic and copies ran while one was open for 35% -> 2% of each run, Pallas kernels for 10% -> 18%
where the time goes in v2:
time: 106 us
  Pallas kernels  65.8 us (62%)
  waiting for transfers between devices  22.8 us (22%)
  starting transfers between devices  9.18 us (9%)
  local copies, waits for them, and re-layouts  7.12 us (7%)
    pallas_call x1, Pallas kernels, energy_call(): pl.pallas_call(energy_kernel, grid_spec=pltpu.PrefetchScalarGridSpec(num_...  26.5 us
    ppermute x1, waiting for transfers between devices, local(): before_a = lax.ppermute(share, 'slab', up)  22.8 us
    pallas_call x1, Pallas kernels, local(): pl.pallas_call(functools.partial(tail_kernel, slabs, probes, cells, types...  19.9 us
    pallas_call x1, Pallas kernels, probe_call(): pl.pallas_call(probe_kernel, grid_spec=pltpu.PrefetchScalarGridSpec(num_s...  19.4 us
    unnamed x26, local copies, waits for them, and re-layouts  5.49 us
    ppermute x1, starting transfers between devices, local(): after_a = lax.ppermute(share, 'slab', down)  5.41 us
    ppermute x1, starting transfers between devices, local(): before_a = lax.ppermute(share, 'slab', up)  2.54 us
  transfers between devices with their start and end apart: 4, of which 1 were waited for; matrix products, arithmetic and copies ran while one was open for 2% of the time, Pallas kernels for 18%

profile of v2, /device:TPU:1, one launch (start us, length us, event | category | flops | bytes accessed | tf_op | source)
XLA Modules:
  0.0 105.9 jit_solution(4769171829868622437)
XLA Ops:
  0.0 0.0 copy-start.6
  0.0 0.0 copy-start.3
  0.0 0.0 copy-start.5
  0.0 0.0 copy-start.1
  0.0 0.0 copy-start.7
  0.0 0.0 copy-start.8
  0.1 1.5 %constant_dynamic-slice_fusion = f32[4,8,64,128]{3,2,1,0:T(8,128)S(1)} fusion(f32[8,8,64,128]{3,2,1,0:T(8,128)} %own_ref.1, s32[]{:T(128)S(6)} %select_n.11), kind=kLoop, calls=%fused_computation.3 | loop fusion | bytes 2097156 | tf_op jit(solution)/shard_map/dynamic_slice | solution.py:661
  1.5 2.5 %collective-permute-start = (f32[4,8,64,128]{3,2,1,0:T(8,128)S(1)}, f32[4,8,64,128]{3,2,1,0:T(8,128)S(1)}, u32[]{:S(2)}, u32[]{:S(2)}) collective-permute-start(f32[4,8,64,128]{3,2,1,0:T(8,128)S(1)} %constant_dynamic-slice_fusion), channel_id=1, source_target_pairs={{0,1},{1,2},{2,3},{3,4},{4,5},{5,6},{6,7},{7,8},{8,9},{9,10},{10,1... | collective-permute-start | bytes 3145736 | tf_op jit(solution)/shard_map/ppermute | solution.py:662
  4.1 5.4 %collective-permute-start.2 = (f32[4,8,64,128]{3,2,1,0:T(8,128)S(1)}, f32[4,8,64,128]{3,2,1,0:T(8,128)}, u32[]{:S(2)}, u32[]{:S(2)}) collective-permute-start(f32[4,8,64,128]{3,2,1,0:T(8,128)S(1)} %constant_dynamic-slice_fusion), channel_id=1, source_target_pairs={{1,0},{2,1},{3,2},{4,3},{5,4},{6,5},{7,6},{8,7},{9,8},{10,9},{11,1... | collective-permute-start | bytes 3145736 | tf_op jit(solution)/shard_map/ppermute | solution.py:663
  9.5 22.8 %collective-permute-done.before_a = f32[4,8,64,128]{3,2,1,0:T(8,128)S(1)} collective-permute-done((f32[4,8,64,128]{3,2,1,0:T(8,128)S(1)}, f32[4,8,64,128]{3,2,1,0:T(8,128)S(1)}, u32[]{:S(2)}, u32[]{:S(2)}) %collective-permute-start) | collective-permute-done | bytes 1048608 | tf_op jit(solution)/shard_map/ppermute | solution.py:662
  32.3 1.2 %collective-permute-start.1 = (f32[4,8,64,128]{3,2,1,0:T(8,128)S(1)}, f32[4,8,64,128]{3,2,1,0:T(8,128)}, u32[]{:S(2)}, u32[]{:S(2)}) collective-permute-start(f32[4,8,64,128]{3,2,1,0:T(8,128)S(1)} %collective-permute-done.before_a), channel_id=1, source_target_pairs={{0,32},{32,0},{64,96},{96,64},{1,33},{33,1},{65,97},{97,65},{2,34}... | collective-permute-start | bytes 3145736 | tf_op jit(solution)/shard_map/ppermute | solution.py:664
  33.5 0.0 collective-permute-done.2.after_a
  33.5 0.0 collective-permute-start.3
  33.5 0.8 copy.18
  34.3 0.1 reshape.9
  34.4 0.9 select_reduce_fusion
  35.2 0.1 pad_add_fusion.scalars
  35.3 0.0 copy-done.6
  35.3 0.0 copy-done.3
  35.3 0.0 copy-done.5
  35.3 0.0 copy-done.1
  35.3 0.0 copy-done.7
  35.3 0.0 copy-done.8
  35.3 0.0 copy-start
  35.4 1.7 %copy-done = f32[16,8,4913]{2,1,0:T(8,128)S(1)} copy-done((f32[16,8,4913]{2,1,0:T(8,128)S(1)}, f32[16,8,4913]{2,1,0:T(8,128)}, u32[]{:S(2)}) %copy-start) | copy-done | bytes 2515480
  37.1 0.0 copy-start.2
  37.1 1.5 %copy-done.2 = bf16[512,1792]{1,0:T(8,128)(2,1)S(1)} copy-done((bf16[512,1792]{1,0:T(8,128)(2,1)S(1)}, bf16[512,1792]{1,0:T(8,128)(2,1)}, u32[]{:S(2)}) %copy-start.2) | copy-done | bytes 1835032
  38.6 0.0 copy-start.4
  38.6 0.8 copy-done.4
  39.4 0.0 copy-start.9
  39.4 0.0 copy-start.10
  39.4 0.0 copy-start.11
  39.4 19.4 %probe_spectra.1 = f32[32,7,128,256]{3,2,1,0:T(8,128)} custom-call(s32[4]{0:T(128)S(1)} %copy-done.7, s32[4]{0:T(128)S(1)} %bitcast.5, s32[1]{0:T(128)} %bitcast.core, s32[24,4]{1,0:T(8,128)S(1)} %copy-done.6, f32[16,8,4913]{2,1,0:T(8,128)S(1)} %copy-done, bf16[384,384]{1,0:T(8,128)(2,1)S(1)} %copy-done.3, s32[8,512]{1,0:T(8,128)S(1)} %copy-done.5, ...), custom_call_target="tpu_custom_call" | custom-call | flops 8589934592 | bytes 41943040 | tf_op jit(solution)/shard_map/probe_spectra/pallas_call | solution.py:222
  58.8 0.0 collective-permute-done.1.before_b
  58.8 0.0 collective-permute-done.3.after_b
  58.8 0.0 copy-done.9
  58.8 0.0 copy-done.10
  58.8 0.0 copy-done.11
  58.8 26.5 %energy_maps.1 = (f32[4,8,64,128]{3,2,1,0:T(8,128)S(1)}, f32[4,8,128]{2,1,0:T(8,128)S(1)}) custom-call(s32[9]{0:T(128)S(1)} %pad_add_fusion.scalars, f32[8,8,64,128]{3,2,1,0:T(8,128)} %own_ref.1, f32[4,8,64,128]{3,2,1,0:T(8,128)S(1)} %collective-permute-done.before_a, f32[4,8,64,128]{3,2,1,0:T(8,128)} %collective-permute-done.1.before_b, ...), custom_call_target="tpu_custom_call" | custom-call | flops 12884901888 | bytes 41943040 | tf_op jit(solution)/shard_map/energy_maps/pallas_call | solution.py:598
  85.3 0.1 broadcast_in_dim.5.weight_ref
  85.4 19.9 %consensus_tail.1 = f32[8,16,128]{2,1,0:T(8,128)S(1)} custom-call(f32[4,8,64,128]{3,2,1,0:T(8,128)S(1)} %get-tuple-element.7.total_ref, f32[4,8,128]{2,1,0:T(8,128)S(1)} %get-tuple-element.8.sum_ref, f32[8,128]{1,0:T(8,128)S(1)} %broadcast_in_dim.5.weight_ref), custom_call_target="tpu_custom_call" | custom-call | tf_op jit(solution)/shard_map/consensus_tail/pallas_call | solution.py:677
  105.3 0.6 copy.20
  (1 shorter events, 0.0 us)
Async XLA Ops:
  0.0 35.3 %copy-start.6 = (s32[24,4]{1,0:T(8,128)S(1)}, s32[24,4]{1,0:T(8,128)}, u32[]{:S(2)}) copy-start(s32[24,4]{1,0:T(8,128)} %constant.46.clone.turns) | copy-start | bytes 1156
  0.0 35.3 %copy-start.3 = (bf16[384,384]{1,0:T(8,128)(2,1)S(1)}, bf16[384,384]{1,0:T(8,128)(2,1)}, u32[]{:S(2)}) copy-start(bf16[384,384]{1,0:T(8,128)(2,1)} %constant.47.clone.swap_ref) | copy-start | bytes 884740
  0.0 35.3 %copy-start.5 = (s32[8,512]{1,0:T(8,128)S(1)}, s32[8,512]{1,0:T(8,128)}, u32[]{:S(2)}) copy-start(s32[8,512]{1,0:T(8,128)} %constant.48.clone.lane_ref) | copy-start | bytes 49156
  0.0 35.3 %copy-start.1 = (bf16[512,1792]{1,0:T(8,128)(2,1)S(1)}, bf16[512,1792]{1,0:T(8,128)(2,1)}, u32[]{:S(2)}) copy-start(bf16[512,1792]{1,0:T(8,128)(2,1)} %constant.49.clone.te_ref) | copy-start | bytes 5505028
  0.0 35.3 %copy-start.7 = (s32[4]{0:T(128)S(1)}, s32[4]{0:T(128)}, u32[]{:S(2)}) copy-start(s32[4]{0:T(128)} %ids.1) | copy-start | bytes 52
  0.0 35.3 %copy-start.8 = (s32[4,1]{0,1:T(1,128)S(1)}, s32[4,1]{0,1:T(1,128)}, u32[]{:S(2)}) copy-start(s32[4,1]{0,1:T(1,128)} %param.18) | copy-start | bytes 52
  1.5 30.7 %collective-permute-start = (f32[4,8,64,128]{3,2,1,0:T(8,128)S(1)}, f32[4,8,64,128]{3,2,1,0:T(8,128)S(1)}, u32[]{:S(2)}, u32[]{:S(2)}) collective-permute-start(f32[4,8,64,128]{3,2,1,0:T(8,128)S(1)} %constant_dynamic-slice_fusion), channel_id=1, source_target_pairs={{0,1},{1,2},{2,3},{3,4},{4,5},{5,6},{6,7},{7,8},{8,9},{9,10},{10,1... | collective-permute-start | bytes 3145736 | tf_op jit(solution)/shard_map/ppermute | solution.py:662
  4.1 29.4 %collective-permute-start.2 = (f32[4,8,64,128]{3,2,1,0:T(8,128)S(1)}, f32[4,8,64,128]{3,2,1,0:T(8,128)}, u32[]{:S(2)}, u32[]{:S(2)}) collective-permute-start(f32[4,8,64,128]{3,2,1,0:T(8,128)S(1)} %constant_dynamic-slice_fusion), channel_id=1, source_target_pairs={{1,0},{2,1},{3,2},{4,3},{5,4},{6,5},{7,6},{8,7},{9,8},{10,9},{11,1... | collective-permute-start | bytes 3145736 | tf_op jit(solution)/shard_map/ppermute | solution.py:663
  32.3 26.5 %collective-permute-start.1 = (f32[4,8,64,128]{3,2,1,0:T(8,128)S(1)}, f32[4,8,64,128]{3,2,1,0:T(8,128)}, u32[]{:S(2)}, u32[]{:S(2)}) collective-permute-start(f32[4,8,64,128]{3,2,1,0:T(8,128)S(1)} %collective-permute-done.before_a), channel_id=1, source_target_pairs={{0,32},{32,0},{64,96},{96,64},{1,33},{33,1},{65,97},{97,65},{2,34}... | collective-permute-start | bytes 3145736 | tf_op jit(solution)/shard_map/ppermute | solution.py:664
  33.5 25.3 %collective-permute-start.3 = (f32[4,8,64,128]{3,2,1,0:T(8,128)}, f32[4,8,64,128]{3,2,1,0:T(8,128)}, u32[]{:S(2)}, u32[]{:S(2)}) collective-permute-start(f32[4,8,64,128]{3,2,1,0:T(8,128)} %collective-permute-done.2.after_a), channel_id=1, source_target_pairs={{0,32},{32,0},{64,96},{96,64},{1,33},{33,1},{65,97},{97,65},{2,34}... | collective-permute-start | bytes 3145736 | tf_op jit(solution)/shard_map/ppermute | solution.py:665
  35.3 1.7 %copy-start = (f32[16,8,4913]{2,1,0:T(8,128)S(1)}, f32[16,8,4913]{2,1,0:T(8,128)}, u32[]{:S(2)}) copy-start(f32[16,8,4913]{2,1,0:T(8,128)} %lib_ref.1) | copy-start | bytes 7546372
  37.1 1.5 %copy-start.2 = (bf16[512,1792]{1,0:T(8,128)(2,1)S(1)}, bf16[512,1792]{1,0:T(8,128)(2,1)}, u32[]{:S(2)}) copy-start(bf16[512,1792]{1,0:T(8,128)(2,1)} %constant.50.clone.to_ref) | copy-start | bytes 5505028
  38.6 0.8 copy-start.4
  39.4 19.4 %copy-start.9 = (bf16[768,256]{1,0:T(8,128)(2,1)S(1)}, bf16[768,256]{1,0:T(8,128)(2,1)}, u32[]{:S(2)}) copy-start(bf16[768,256]{1,0:T(8,128)(2,1)} %constant.53.clone.wf_ref) | copy-start | bytes 1179652
  39.4 19.4 %copy-start.10 = (bf16[768,256]{1,0:T(8,128)(2,1)S(1)}, bf16[768,256]{1,0:T(8,128)(2,1)}, u32[]{:S(2)}) copy-start(bf16[768,256]{1,0:T(8,128)(2,1)} %constant.54.clone.wi_ref) | copy-start | bytes 1179652
  39.4 19.4 %copy-start.11 = (bf16[128,192]{1,0:T(8,128)(2,1)S(1)}, bf16[128,192]{1,0:T(8,128)(2,1)}, u32[]{:S(2)}) copy-start(bf16[128,192]{1,0:T(8,128)(2,1)} %constant.52.clone.tz_ref) | copy-start | bytes 147460

commit v3 on v2

v3 whole, which is shorter than its diff:
```python
import functools
import math

import jax
import jax.numpy as jnp
import ml_dtypes
import numpy as np
from jax import lax
from jax.experimental import pallas as pl
from jax.experimental.pallas import tpu as pltpu
from jax.sharding import PartitionSpec as P

RAD = 8
KS = 17
AZ = 24
EXT = 24
KX = 13
PAIRS = 7
NZ = 64
NY = 128
ENERGY_CAP = 6.0
HIGHEST = lax.Precision.HIGHEST
MESH = pl.DeviceIdType.MESH
BF = jnp.bfloat16
F32 = jnp.float32


def cube_rotations():
    permutes = [(0, 1, 2), (0, 2, 1), (1, 0, 2), (1, 2, 0), (2, 0, 1), (2, 1, 0)]
    parities = [1, -1, -1, 1, 1, -1]
    perms, signs = [], []
    for permute, parity in zip(permutes, parities):
        for sign_x in (1, -1):
            for sign_y in (1, -1):
                for sign_z in (1, -1):
                    if parity * sign_x * sign_y * sign_z == 1:
                        perms.append(permute)
                        signs.append((sign_x, sign_y, sign_z))
    return np.array(perms, np.int32), np.array(signs, np.int32)


def split_np(table):
    table = table.astype(np.float32)
    hi = table.astype(ml_dtypes.bfloat16)
    lo = (table - hi.astype(np.float32)).astype(ml_dtypes.bfloat16)
    return hi, lo


HALF = (KS * KS + 1) // 2
CUBE = 384
PACK = 512


def half_offsets():
    flat = np.arange(HALF) + HALF - 1
    return flat // KS - RAD, flat % KS - RAD


def xy_tables():
    ax, ay = half_offsets()
    kx = np.arange(2 * PAIRS)
    ky = np.arange(NY)
    px = (ax[:, None] * kx[None, :]) % EXT / EXT
    py = (ay[:, None] * ky[None, :]) % NY / NY
    ang = 2 * np.pi * (px[:, :, None] + py[:, None, :])
    live = (kx < KX).astype(np.float64)[None, :, None]
    out = []
    for t in (np.cos(ang) * live, np.sin(ang) * live):
        hi, lo = split_np(t.reshape(HALF, -1))
        pad = np.zeros((PACK - 3 * HALF, hi.shape[1]), hi.dtype)
        out.append(np.concatenate([hi, hi, lo, pad], axis=0))
    return out


def lane_offsets():
    ax, ay = half_offsets()
    rows = np.full((8, PACK), 10000, np.int32)
    for c in range(3):
        rows[0, c * HALF : (c + 1) * HALF] = ax
        rows[1, c * HALF : (c + 1) * HALF] = ay
    rows[2] = 0
    rows[2, [0, HALF, 2 * HALF]] = 10000
    return rows


def swap_table():
    t = np.zeros((CUBE, CUBE), np.float32)
    for m in range(KS):
        for n in range(KS):
            t[n * KS + m, m * KS + n] = 1
    return t.astype(ml_dtypes.bfloat16)


def rotation_table():
    perms, signs = cube_rotations()
    table = np.zeros((24, 4), np.int32)
    for q in range(24):
        zaxis = [i for i in range(3) if perms[q, i] == 2][0]
        others = [i for i in range(3) if i != zaxis]
        table[q, 0] = zaxis
        table[q, 1] = 1 if signs[q, zaxis] < 0 else 0
        for i, unit in zip(others, (KS, 1)):
            table[q, 2 + perms[q, i]] = unit * signs[q, i]
    return table


def probe_z_steps():
    kz = np.arange(2 * NZ) % NZ
    lane = np.arange(6 * AZ) % (2 * AZ)
    az = lane % AZ
    quarter = np.where((np.arange(2 * NZ) < NZ)[:, None], np.where(lane < AZ, 0, 16), np.where(lane < AZ, -16, 0))
    turn = (kz[:, None] * (az - RAD)[None, :] + quarter) % NZ
    live = np.broadcast_to((az < KS).astype(np.int64)[None], turn.shape)
    return np.stack([turn, np.broadcast_to(kz[:, None], turn.shape), live]).astype(np.int32)


def grid_z_table():
    k = np.arange(NZ)
    ang = 2 * np.pi * ((k[:, None] * k[None, :]) % NZ) / NZ
    t = np.concatenate([np.cos(ang), np.sin(ang)], axis=0)
    hi, lo = split_np(t)
    return np.concatenate([hi, lo, hi], axis=1)


def grid_y_table(direction):
    k = np.arange(NY)
    ang = 2 * np.pi * ((k[:, None] * k[None, :]) % NY) / NY
    c, s = np.cos(ang), direction * np.sin(ang)
    hi, lo = split_np(np.block([[c, s], [-s, c]]))
    return np.concatenate([hi, hi, lo], axis=0)


def split(x):
    hi = x.astype(BF)
    lo = (x - hi.astype(F32)).astype(BF)
    return hi, lo


def turned_probes(ids, rots, offs, turns, core, lib_ref, swap_ref, lane_ref, zstep_ref, xa, xb, kd, even, odd, tzs, ph):
    slots, terms = tzs.shape[0], lib_ref.shape[1]
    xa[...] = jnp.zeros_like(xa)
    kd[...] = jnp.zeros_like(kd)
    lane = lax.broadcasted_iota(jnp.int32, (terms, CUBE), 1)
    packed_lane = lax.broadcasted_iota(jnp.int32, (terms * AZ, 128), 1)
    source = lax.broadcasted_iota(jnp.int32, (CUBE, PACK), 0)
    zlane = lax.broadcasted_iota(jnp.int32, (2 * NZ, 6 * AZ), 1)
    ky = lax.broadcasted_iota(jnp.int32, (8, 2 * NY), 1) % NY

    def permuted(x, table):
        hi, lo = split(x)
        out = jnp.dot(jnp.concatenate([hi, lo], axis=0), table, preferred_element_type=F32)
        return out[: x.shape[0]] + out[x.shape[0] :]

    @pl.loop(0, slots)
    def _(slot):
        rot = rots[slot]
        zaxis, flipped = turns[rot, 0], turns[rot, 1]
        step_x, step_y = turns[rot, 2], turns[rot, 3]
        off_y, off_z = offs[2 * slot], offs[2 * slot + 1]

        turn = (zstep_ref[0] - zstep_ref[1] * off_z + NZ * NZ) & (NZ - 1)
        t = jnp.cos(turn.astype(F32) * (2 * math.pi / NZ)) * zstep_ref[2].astype(F32)
        hi, lo = split(t)
        tzs[slot] = jnp.where((zlane >= 2 * AZ) & (zlane < 4 * AZ), lo.astype(F32), hi.astype(F32)).astype(BF)
        turn = ky * off_y
        ph[slot, 0] = jnp.cos((turn & (NY - 1)).astype(F32) * (2 * math.pi / NY))
        ph[slot, 1] = jnp.cos(((turn - NY // 4) & (NY - 1)).astype(F32) * (2 * math.pi / NY))

        for m in range(KS):
            w = lib_ref[ids[slot], :, m * KS * KS : (m + 1) * KS * KS]
            xa[m, :, : KS * KS] = jnp.where(core == 0, w, pltpu.roll(w, terms // 2, 0))
        x = xa[...]
        swapped = permuted(x.reshape(KS * terms, CUBE), swap_ref[...]).reshape(KS, terms, CUBE)
        xa[...] = jnp.where(zaxis == 2, swapped, x)
        for m in range(KS):
            acc = jnp.zeros((terms, CUBE), F32)
            for n in range(KS):
                moved = pltpu.roll(xa[n], ((n - m) * KS) % CUBE, 1)
                acc = jnp.where((lane >= n * KS) & (lane < (n + 1) * KS), moved, acc)
            xb[m] = jnp.where(zaxis == 0, xa[m], acc)

        here = lane_ref[0:1] * step_x + lane_ref[1:2] * step_y + (HALF - 1)
        there = 2 * (HALF - 1) - here + lane_ref[2:3]
        plus = (source == here).astype(F32)
        minus = (source == there).astype(F32)
        x = xb[...].reshape(KS * terms, CUBE)
        for table, ref in ((plus + minus, even), (plus - minus, odd)):
            turned = permuted(x, table.astype(BF))
            for m in range(KS):
                f = KS - 1 - m
                row = jnp.where(flipped == 1, turned[f * terms : (f + 1) * terms], turned[m * terms : (m + 1) * terms])
                for j in range(PACK // 128):
                    kd[j, pl.ds(m, terms, stride=AZ), :] = row[:, j * 128 : (j + 1) * 128]
            rows = pl.ds(pl.multiple_of(slot * terms * AZ, terms * AZ), terms * AZ)
            for j in range(PACK // 128):
                hi, lo = split(kd[j])
                packed = packed_lane + j * 128
                low = (packed >= HALF) & (packed < 2 * HALF)
                ref[rows, j * 128 : (j + 1) * 128] = jnp.where(low, lo.astype(F32), hi.astype(F32)).astype(BF)


def probe_pair(p, te, to, even, odd, tzs, ph, q):
    slots, terms = q.shape[0], q.shape[1]
    columns = pl.ds(pl.multiple_of(p * 2 * NY, 2 * NY), 2 * NY)
    re_all = jnp.dot(even[...], te[:, columns], preferred_element_type=F32)
    im_all = jnp.dot(odd[...], to[:, columns], preferred_element_type=F32)
    for s in range(slots):
        c, n = ph[s, 0, 0:1], ph[s, 1, 0:1]
        rows = slice(s * terms * AZ, (s + 1) * terms * AZ)
        re = re_all[rows] * c + im_all[rows] * n
        im = im_all[rows] * c - re_all[rows] * n
        tz = tzs[s]
        for t in range(terms):
            d = jnp.concatenate([re[t * AZ : (t + 1) * AZ], im[t * AZ : (t + 1) * AZ]], axis=0)
            hi, lo = split(d)
            q[s, t, p] = jnp.dot(tz, jnp.concatenate([hi, hi, lo], axis=0), preferred_element_type=F32)


def cos24(m):
    return math.cos(2 * math.pi * (m % 24) / 24)


def sin24(m):
    return math.sin(2 * math.pi * (m % 24) / 24)


def lin(terms):
    total = None
    for coef, value in terms:
        if abs(coef) < 1e-12:
            continue
        if abs(coef - 1) < 1e-12:
            total = value if total is None else total + value
        elif abs(coef + 1) < 1e-12:
            total = -value if total is None else total - value
        else:
            total = coef * value if total is None else total + coef * value
    return total


def real_dft24(r):
    a = [r[0]] + [r[n] + r[24 - n] for n in range(1, 12)] + [r[12]]
    b = [None] + [r[n] - r[24 - n] for n in range(1, 12)]
    re, im = [None] * 13, [None] * 13
    c = [a[n] + a[12 - n] for n in range(6)] + [a[6]]
    d = [a[n] - a[12 - n] for n in range(6)]
    ce = [c[n] + c[6 - n] for n in range(3)] + [c[3]]
    co = [c[n] - c[6 - n] for n in range(3)]
    for m in range(7):
        if m % 2 == 0:
            re[2 * m] = lin([(cos24(2 * m * n), ce[n]) for n in range(4)])
        else:
            re[2 * m] = lin([(cos24(2 * m * n), co[n]) for n in range(3)])
    for k in range(1, 12, 2):
        re[k] = lin([(cos24(k * n), d[n]) for n in range(6)])
    e = [None] + [b[n] + b[12 - n] for n in range(1, 6)] + [b[6]]
    f = [None] + [b[n] - b[12 - n] for n in range(1, 6)]
    for k in range(1, 12, 2):
        im[k] = lin([(-sin24(k * n), e[n]) for n in range(1, 7)])
    fo = [None] + [f[n] + f[6 - n] for n in range(1, 3)] + [f[3]]
    fe = [None] + [f[n] - f[6 - n] for n in range(1, 3)]
    for m in range(1, 6):
        if m % 2 == 1:
            im[2 * m] = lin([(-sin24(2 * m * n), fo[n]) for n in range(1, 4)])
        else:
            im[2 * m] = lin([(-sin24(2 * m * n), fe[n]) for n in range(1, 3)])
    return re, im


def y_stage(x, w):
    hi, lo = split(x)
    return jnp.dot(jnp.concatenate([hi, lo, hi], axis=1), w, preferred_element_type=F32)


def z_stage(tz, x, direction):
    hi, lo = split(x)
    rhs = jnp.concatenate([hi, hi, lo], axis=0)
    p = jnp.dot(tz, rhs, preferred_element_type=F32)
    re = p[:NZ, :NY] - direction * p[NZ:, NY:]
    im = p[:NZ, NY:] + direction * p[NZ:, :NY]
    return re, im


def forward(i, own, before, after, wf_ref, tz, work, spec):
    @pl.loop(0, 8)
    def _(chunk):
        rows = pl.ds(pl.multiple_of(chunk * 8, 8), 8)
        r = (
            [before[i, n, rows] for n in range(8)]
            + [own[i, n, rows] for n in range(8)]
            + [after[i, n, rows] for n in range(8)]
        )
        re, im = real_dft24(r)
        for k in range(KX):
            work[k, rows, :NY] = re[k]
            work[k, rows, NY:] = im[k] if im[k] is not None else jnp.zeros_like(re[k])

    y = y_stage(work[...].reshape(KX * NZ, 2 * NY), wf_ref[...])
    work[...] = y.reshape(KX, NZ, 2 * NY)
    for k in range(KX):
        re, im = z_stage(tz, work[k], -1.0)
        spec[i, k, :, :NY] = re
        spec[i, k, :, NY:] = im


def boltzmann(slot, q, wi_ref, tz, work, spec, total_ref, sum_ref):
    @pl.loop(0, 8)
    def _(chunk):
        start = pl.multiple_of(chunk * 8, 8)
        rows = pl.ds(start, 8)
        low = pl.ds(start + NZ, 8)
        for k in range(KX):
            p, lane = k // 2, (k % 2) * NY
            re = im = None
            for t in range(8):
                gr, gi = spec[t, k, rows, :NY], spec[t, k, rows, NY:]
                qr = q[slot, t, p, rows, lane : lane + NY]
                qi = q[slot, t, p, low, lane : lane + NY]
                tr = gr * qr - gi * qi
                ti = gr * qi + gi * qr
                re = tr if re is None else re + tr
                im = ti if im is None else im + ti
            work[k, rows, :NY] = re
            work[k, rows, NY:] = im

    for k in range(KX):
        re, im = z_stage(tz, work[k], 1.0)
        work[k, :, :NY] = re
        work[k, :, NY:] = im
    y = y_stage(work[...].reshape(KX * NZ, 2 * NY), wi_ref[...])
    work[...] = y.reshape(KX, NZ, 2 * NY)
    sum_ref[slot] = jnp.zeros((8, NY), F32)
    scale = 1.0 / (EXT * NZ * NY)

    @pl.loop(0, 8)
    def _(chunk):
        rows = pl.ds(pl.multiple_of(chunk * 8, 8), 8)
        fr = [work[k, rows, :NY] for k in range(KX)]
        fi = [work[k, rows, NY:] for k in range(KX)]
        acc = sum_ref[slot]
        for m in range(5):
            even, odd = [], []
            for k in range(KX):
                w = scale * (1.0 if k in (0, 12) else 2.0) * (-1) ** k
                even.append((w * cos24(k * m), fr[k]))
                odd.append((w * sin24(k * m), fi[k]))
            even, odd = sum_terms(even), sum_terms(odd)
            for x, e in ((4, even),) if m == 0 else ((4 + m, even - odd), (4 - m, even + odd)):
                if x < 8:
                    b = jnp.exp(-ENERGY_CAP * jnp.tanh(e / ENERGY_CAP))
                    total_ref[slot, x, rows] = b
                    acc = acc + b
        sum_ref[slot] = acc


def energy_kernel(
    slabs,
    ids,
    rots,
    offs,
    turns,
    receptor,
    library,
    te_hbm,
    to_hbm,
    swap_ref,
    lane_ref,
    zstep_ref,
    tz_ref,
    wf_ref,
    wi_ref,
    total_ref,
    sum_ref,
    lib,
    te,
    to,
    own,
    before,
    after,
    xa,
    xb,
    kd,
    even,
    odd,
    tzs,
    ph,
    q,
    spec,
    work,
    send,
    recv,
    hand_send,
    hand_recv,
    near,
):
    terms = receptor.shape[0]
    half = terms // 2
    slots = total_ref.shape[0]
    slab = lax.axis_index("slab")
    probe = lax.axis_index("probe")
    core = lax.rem(probe, 2)
    right = {"slab": lax.rem(slab + 1, slabs)}
    left = {"slab": lax.rem(slab + slabs - 1, slabs)}
    other = {"probe": probe + 1 - 2 * core}

    barrier = pltpu.get_barrier_semaphore()
    for device in (left, right, other):
        pl.semaphore_signal(barrier, inc=1, device_id=device, device_id_type=MESH)
    nearby = [
        pltpu.make_async_copy(library, lib, near.at[0]),
        pltpu.make_async_copy(te_hbm, te, near.at[1]),
        pltpu.make_async_copy(to_hbm, to, near.at[2]),
        pltpu.make_async_copy(receptor.at[pl.ds(core * half, half)], own.at[pl.ds(0, half)], near.at[3]),
        pltpu.make_async_copy(receptor.at[pl.ds((1 - core) * half, half)], own.at[pl.ds(half, half)], near.at[4]),
    ]
    pl.semaphore_wait(barrier, 3)

    def halo_copy(j, side):
        return pltpu.make_async_remote_copy(
            src_ref=receptor.at[core * half + j],
            dst_ref=(before, after)[side].at[j],
            send_sem=send.at[side, j],
            recv_sem=recv.at[side, j],
            device_id=(right, left)[side],
            device_id_type=MESH,
        )

    def hand_copy(j, side):
        ref = (before, after)[side]
        return pltpu.make_async_remote_copy(
            src_ref=ref.at[j],
            dst_ref=ref.at[half + j],
            send_sem=hand_send.at[side, j],
            recv_sem=hand_recv.at[side, j],
            device_id=other,
            device_id_type=MESH,
        )

    def hand_over(j):
        for side in range(2):
            halo_copy(j, side).wait_recv()
            hand_copy(j, side).start()

    for j in range(half):
        for side in range(2):
            halo_copy(j, side).start()
    for copy in nearby:
        copy.start()
    nearby[0].wait()
    turned_probes(ids, rots, offs, turns, core, lib, swap_ref, lane_ref, zstep_ref, xa, xb, kd, even, odd, tzs, ph)
    for copy in nearby[1:]:
        copy.wait()

    def pairs(low, high):
        @pl.loop(low, high)
        def _(p):
            probe_pair(p, te, to, even, odd, tzs, ph, q)

    pairs(0, 3)
    hand_over(0)
    pairs(3, PAIRS)
    hand_over(1)
    tz = tz_ref[...]

    @pl.loop(0, half)
    def _(j):
        @pl.when(j >= 2)
        def _():
            hand_over(j)

        @pl.loop(0, 2)
        def _(h):
            @pl.when(h == 1)
            def _():
                for side in range(2):
                    hand_copy(j, side).wait_recv()

            forward(j + half * h, own, before, after, wf_ref, tz, work, spec)

    @pl.loop(0, slots)
    def _(slot):
        boltzmann(slot, q, wi_ref, tz, work, spec, total_ref, sum_ref)

    @pl.loop(0, half)
    def _(j):
        for side in range(2):
            halo_copy(j, side).wait_send()
            hand_copy(j, side).wait_send()


def sum_terms(terms):
    total = None
    for coef, value in terms:
        if abs(coef) < 1e-15:
            continue
        total = coef * value if total is None else total + coef * value
    return total


def tail_kernel(
    slabs,
    probes,
    cells,
    types,
    total_ref,
    sum_ref,
    weight_ref,
    out_ref,
    mine,
    gathered,
    halo,
    mixed,
    blocks,
    part_send,
    part_recv,
    halo_send,
    halo_recv,
    block_send,
    block_recv,
):
    slots = total_ref.shape[0]
    planes = total_ref.shape[1]
    rows = out_ref.shape[1]
    slab = lax.axis_index("slab")
    probe = lax.axis_index("probe")

    barrier = pltpu.get_barrier_semaphore()

    @pl.loop(1, slabs)
    def _(d):
        pl.semaphore_signal(
            barrier, inc=1, device_id={"slab": lax.rem(slab + d, slabs)}, device_id_type=MESH
        )

    for d in range(1, probes):
        pl.semaphore_signal(
            barrier, inc=1, device_id={"probe": lax.rem(probe + d, probes)}, device_id_type=MESH
        )

    parts = []
    for s in range(slots):
        v = jnp.sum(sum_ref[s], axis=0, keepdims=True)
        v = jnp.sum(v, axis=1, keepdims=True)
        parts.append(jnp.broadcast_to(v, (1, NY)))
    parts += [jnp.zeros((1, NY), F32)] * (8 - slots)
    own = jnp.concatenate(parts, axis=0)
    mine[...] = own

    pl.semaphore_wait(barrier, slabs - 1 + probes - 1)

    def part_copy(d):
        return pltpu.make_async_remote_copy(
            src_ref=mine,
            dst_ref=gathered.at[d],
            send_sem=part_send.at[d],
            recv_sem=part_recv.at[d],
            device_id={"slab": lax.rem(slab + d, slabs)},
            device_id_type=MESH,
        )

    @pl.loop(1, slabs)
    def _(d):
        part_copy(d).start()

    to_right = pltpu.make_async_remote_copy(
        src_ref=total_ref.at[:, planes - 1],
        dst_ref=halo.at[0],
        send_sem=halo_send.at[0],
        recv_sem=halo_recv.at[0],
        device_id={"slab": lax.rem(slab + 1, slabs)},
        device_id_type=MESH,
    )
    to_left = pltpu.make_async_remote_copy(
        src_ref=total_ref.at[:, 0],
        dst_ref=halo.at[1],
        send_sem=halo_send.at[1],
        recv_sem=halo_recv.at[1],
        device_id={"slab": lax.rem(slab + slabs - 1, slabs)},
        device_id_type=MESH,
    )
    to_right.start()
    to_left.start()

    @pl.loop(1, slabs)
    def _(d):
        part_copy(d).wait_recv()

    partition = own
    for d in range(1, slabs):
        partition = partition + gathered[d]
    coef = weight_ref[...] * (cells / partition)
    coefs = [jnp.broadcast_to(coef[s : s + 1], (8, NY)) for s in range(slots)]

    def weighted(read):
        total = None
        for s in range(slots):
            v = read(s).reshape(NZ // 8, 8, NY) * coefs[s][None]
            total = v if total is None else total + v
        return total.reshape(NZ, NY)

    to_right.wait_recv()
    to_left.wait_recv()
    mixed[0] = weighted(lambda s: halo[0, s])
    mixed[planes + 1] = weighted(lambda s: halo[1, s])
    for x in range(planes):
        mixed[x + 1] = weighted(lambda s: total_ref[s, x])
    for x in range(planes):
        v = (mixed[x] + 2.0 * mixed[x + 1] + mixed[x + 2]) * 0.25
        v = (pltpu.roll(v, 1, 0) + 2.0 * v + pltpu.roll(v, NZ - 1, 0)) * 0.25
        v = (pltpu.roll(v, 1, 1) + 2.0 * v + pltpu.roll(v, NY - 1, 1)) * 0.25
        mixed[x] = v

    def block_copy(d):
        target = lax.rem(probe + d, probes)
        return pltpu.make_async_remote_copy(
            src_ref=mixed.at[pl.ds(0, planes), pl.ds(pl.multiple_of(target * rows, 8), rows)],
            dst_ref=blocks.at[d - 1],
            send_sem=block_send.at[d - 1],
            recv_sem=block_recv.at[d - 1],
            device_id={"probe": target},
            device_id_type=MESH,
        )

    for d in range(1, probes):
        block_copy(d).start()
    result = mixed[pl.ds(0, planes), pl.ds(pl.multiple_of(probe * rows, 8), rows)]
    for d in range(1, probes):
        block_copy(d).wait_recv()
        result = result + blocks[d - 1]
    out_ref[...] = result * (1.0 / types)

    @pl.loop(1, slabs)
    def _(d):
        part_copy(d).wait_send()

    to_right.wait_send()
    to_left.wait_send()
    for d in range(1, probes):
        block_copy(d).wait_send()


def energy_call(slabs, receptor, library, probe_ids, rotations, offsets):
    terms, planes, nz, ny = receptor.shape
    slots, half = probe_ids.shape[0], terms // 2
    te, to = xy_tables()
    smem = pl.BlockSpec(memory_space=pltpu.SMEM)
    vmem = pl.BlockSpec(memory_space=pltpu.VMEM)
    hbm = pl.BlockSpec(memory_space=pl.ANY)
    dma = pltpu.SemaphoreType.DMA
    return pl.pallas_call(
        functools.partial(energy_kernel, slabs),
        in_specs=[smem] * 4 + [hbm] * 4 + [vmem] * 6,
        out_specs=[vmem, vmem],
        out_shape=[
            jax.ShapeDtypeStruct((slots, planes, nz, ny), F32),
            jax.ShapeDtypeStruct((slots, 8, ny), F32),
        ],
        scratch_shapes=[
            pltpu.VMEM(library.shape, F32),
            pltpu.VMEM(te.shape, BF),
            pltpu.VMEM(to.shape, BF),
            pltpu.VMEM(receptor.shape, F32),
            pltpu.VMEM(receptor.shape, F32),
            pltpu.VMEM(receptor.shape, F32),
            pltpu.VMEM((KS, terms, CUBE), F32),
            pltpu.VMEM((KS, terms, CUBE), F32),
            pltpu.VMEM((PACK // 128, terms * AZ, 128), F32),
            pltpu.VMEM((slots * terms * AZ, PACK), BF),
            pltpu.VMEM((slots * terms * AZ, PACK), BF),
            pltpu.VMEM((slots, 2 * NZ, 6 * AZ), BF),
            pltpu.VMEM((slots, 2, 8, 2 * NY), F32),
            pltpu.VMEM((slots, terms, PAIRS, 2 * NZ, 2 * NY), F32),
            pltpu.VMEM((terms, KX, nz, 2 * ny), F32),
            pltpu.VMEM((KX, nz, 2 * ny), F32),
            dma((2, half)),
            dma((2, half)),
            dma((2, half)),
            dma((2, half)),
            dma((5,)),
        ],
        compiler_params=pltpu.CompilerParams(
            collective_id=1, has_side_effects=True, vmem_limit_bytes=63 << 20
        ),
        name="energy_maps",
    )(
        probe_ids,
        rotations,
        offsets,
        jnp.asarray(rotation_table()),
        receptor,
        library,
        jnp.asarray(te),
        jnp.asarray(to),
        jnp.asarray(swap_table()),
        jnp.asarray(lane_offsets()),
        jnp.asarray(probe_z_steps()),
        jnp.asarray(grid_z_table()),
        jnp.asarray(grid_y_table(-1.0)),
        jnp.asarray(grid_y_table(1.0)),
    )


def local(receptor, library, probe_ids, rotations, offsets, probe_weight):
    terms, planes, nz, ny = receptor.shape
    slabs = lax.axis_size("slab")
    probes = lax.axis_size("probe")
    slots = probe_ids.shape[0]
    types = probe_weight.shape[0]
    cells = float(planes * slabs * nz * ny)

    total, sums = energy_call(
        slabs, receptor, library, probe_ids, rotations.reshape(-1), offsets.reshape(-1)
    )

    onehot = (probe_ids[:, None] == jnp.arange(types, dtype=jnp.int32)[None, :]).astype(F32)
    chosen = jnp.sum(onehot * probe_weight[None], axis=1)
    weight = jnp.broadcast_to(jnp.pad(chosen, (0, 8 - slots))[:, None], (8, ny))
    rows = nz // probes
    vmem = pl.BlockSpec(memory_space=pltpu.VMEM)
    return pl.pallas_call(
        functools.partial(tail_kernel, slabs, probes, cells, types),
        in_specs=[vmem] * 3,
        out_specs=vmem,
        out_shape=jax.ShapeDtypeStruct((planes, rows, ny), F32),
        scratch_shapes=[
            pltpu.VMEM((8, ny), F32),
            pltpu.VMEM((slabs, 8, ny), F32),
            pltpu.VMEM((2, slots, nz, ny), F32),
            pltpu.VMEM((planes + 2, nz, ny), F32),
            pltpu.VMEM((probes - 1, planes, rows, ny), F32),
            pltpu.SemaphoreType.DMA((slabs,)),
            pltpu.SemaphoreType.DMA((slabs,)),
            pltpu.SemaphoreType.DMA((2,)),
            pltpu.SemaphoreType.DMA((2,)),
            pltpu.SemaphoreType.DMA((probes - 1,)),
            pltpu.SemaphoreType.DMA((probes - 1,)),
        ],
        compiler_params=pltpu.CompilerParams(
            collective_id=0, has_side_effects=True, vmem_limit_bytes=24 << 20
        ),
        name="consensus_tail",
    )(total, sums, weight)


def solution(mesh):
    in_specs = (
        P(None, "slab", None, None),
        P(),
        P("probe"),
        P("probe", None),
        P("probe", None, None),
        P(),
    )
    out_specs = P("slab", "probe", None)
    return jax.shard_map(local, mesh=mesh, in_specs=in_specs, out_specs=out_specs, check_vma=False)
```

time: 106 us -> 74.2 us (0.70)
  waiting for transfers between devices: 22.8 us -> 0 us
  starting transfers between devices: 9.18 us -> 0 us
  Pallas kernels: 65.8 us -> 69.1 us
  local copies, waits for them, and re-layouts: 7.12 us -> 4 us
    ppermute x4 -> x0, waiting for transfers between devices: 22.8 us -> none  [the longest x1 22.8 us: local(): before_a = lax.ppermute(share, 'slab', up)]
    ppermute x4 -> x0, starting transfers between devices: 9.18 us -> none  [the longest x1 5.41 us: local(): after_a = lax.ppermute(share, 'slab', down)]
    pallas_call x2 -> x1, Pallas kernels: 45.8 us -> 50.8 us  [energy_call(): pl.pallas_call(functools.partial(energy_kernel, slabs), in_specs=[smem] *...]
    unnamed x26 -> x6, local copies, waits for them, and re-layouts: 5.49 us -> 3.33 us
    pallas_call x1, Pallas kernels: 19.9 us -> 18.3 us  [local(): pl.pallas_call(functools.partial(tail_kernel, slabs, probes, cells, types...]
    dynamic_slice x1 -> x0, local copies, waits for them, and re-layouts: 1.47 us -> none  [local(): share = lax.dynamic_slice_in_dim(receptor, core * half, half, axis=0)]
  transfers between devices with their start and end apart: 4 -> 0, of which waited for: 1 -> 0; matrix products, arithmetic and copies ran while one was open for 2% -> 0% of each run, Pallas kernels for 18% -> 0%
where the time goes in v3:
time: 74.2 us; the launch traced here: 74 us
  Pallas kernels  69.1 us (93%)
  local copies, waits for them, and re-layouts  4 us (5%)
  other arithmetic  0.85 us (1%)
    pallas_call x1, Pallas kernels, energy_call(): pl.pallas_call(functools.partial(energy_kernel, slabs), in_specs=[smem] *...  50.8 us
    pallas_call x1, Pallas kernels, local(): pl.pallas_call(functools.partial(tail_kernel, slabs, probes, cells, types...  18.3 us
    unnamed x6, local copies, waits for them, and re-layouts  3.33 us

profile of v3, /device:TPU:1, one launch (start us, length us, event | category | flops | bytes accessed | tf_op | source)
XLA Modules:
  0.0 74.0 jit_solution(7869222602860998754)
XLA Ops:
  0.0 0.9 %select_reduce_fusion = f32[4]{0:T(128)S(1)} fusion(f32[16]{0:T(128)} %param.20, s32[4]{0:T(128)} %ids.1), kind=kLoop, calls=%fused_computation | loop fusion | flops 188 | bytes 96 | tf_op jit(solution)/shard_map/reduce_sum | solution.py:716
  0.9 0.8 %copy.18 = s32[4,1,2]{2,0,1:T(4,128)S(1)} copy(s32[4,1,2]{0,2,1:T(2,128)} %param.19) | data formatting | bytes 64 | tf_op args[4]
  1.6 0.6 reshape.10.offs
  2.2 0.1 broadcast_in_dim.2.weight_ref
  2.3 50.8 %energy_maps.1 = (f32[4,8,64,128]{3,2,1,0:T(8,128)}, f32[4,8,128]{2,1,0:T(8,128)}) custom-call(s32[4]{0:T(128)} %ids.1, s32[4]{0:T(128)} %bitcast.3, s32[8]{0:T(128)} %reshape.10.offs, s32[24,4]{1,0:T(8,128)} %constant.23.clone.turns, f32[8,8,64,128]{3,2,1,0:T(8,128)} %receptor.1, f32[16,8,4913]{2,1,0:T(8,128)} %library.1, ...), custom_call_target="tpu_custom_call" | custom-call | tf_op jit(solution)/shard_map/energy_maps/pallas_call | solution.py:650
  53.1 0.0 copy-start
  53.1 1.2 %copy-done = f32[4,8,64,128]{3,2,1,0:T(8,128)S(1)} copy-done((f32[4,8,64,128]{3,2,1,0:T(8,128)S(1)}, f32[4,8,64,128]{3,2,1,0:T(8,128)}, u32[]{:S(2)}) %copy-start) | copy-done | bytes 1048600
  54.3 0.0 copy-start.1
  54.3 0.7 copy-done.1
  55.0 18.3 %consensus_tail.1 = f32[8,16,128]{2,1,0:T(8,128)S(1)} custom-call(f32[4,8,64,128]{3,2,1,0:T(8,128)S(1)} %copy-done, f32[4,8,128]{2,1,0:T(8,128)S(1)} %copy-done.1, f32[8,128]{1,0:T(8,128)S(1)} %broadcast_in_dim.2.weight_ref), custom_call_target="tpu_custom_call" | custom-call | tf_op jit(solution)/shard_map/consensus_tail/pallas_call | solution.py:720
  73.3 0.6 copy.20
  (1 shorter events, 0.0 us)
Async XLA Ops:
  53.1 1.2 %copy-start = (f32[4,8,64,128]{3,2,1,0:T(8,128)S(1)}, f32[4,8,64,128]{3,2,1,0:T(8,128)}, u32[]{:S(2)}) copy-start(f32[4,8,64,128]{3,2,1,0:T(8,128)} %get-tuple-element.7.total_ref) | copy-start | bytes 3145732
  54.3 0.7 copy-start.1

commit v4 on v3

--- a/solution.py
+++ b/solution.py
@@ -153,10 +153,10 @@
 
     @pl.loop(0, slots)
     def _(slot):
-        rot = rots[slot]
+        rot = rots[slot, 0]
         zaxis, flipped = turns[rot, 0], turns[rot, 1]
         step_x, step_y = turns[rot, 2], turns[rot, 3]
-        off_y, off_z = offs[2 * slot], offs[2 * slot + 1]
+        off_y, off_z = offs[slot, 0, 0], offs[slot, 0, 1]
 
         turn = (zstep_ref[0] - zstep_ref[1] * off_z + NZ * NZ) & (NZ - 1)
         t = jnp.cos(turn.astype(F32) * (2 * math.pi / NZ)) * zstep_ref[2].astype(F32)
@@ -303,7 +303,7 @@
         spec[i, k, :, NY:] = im
 
 
-def boltzmann(slot, q, wi_ref, tz, work, spec, total_ref, sum_ref):
+def contract(slot, group, q, spec, source, target):
     @pl.loop(0, 8)
     def _(chunk):
         start = pl.multiple_of(chunk * 8, 8)
@@ -311,8 +311,9 @@
         low = pl.ds(start + NZ, 8)
         for k in range(KX):
             p, lane = k // 2, (k % 2) * NY
-            re = im = None
-            for t in range(8):
+            re = None if source is None else source[k, rows, :NY]
+            im = None if source is None else source[k, rows, NY:]
+            for t in group:
                 gr, gi = spec[t, k, rows, :NY], spec[t, k, rows, NY:]
                 qr = q[slot, t, p, rows, lane : lane + NY]
                 qi = q[slot, t, p, low, lane : lane + NY]
@@ -320,9 +321,11 @@
                 ti = gr * qi + gi * qr
                 re = tr if re is None else re + tr
                 im = ti if im is None else im + ti
-            work[k, rows, :NY] = re
-            work[k, rows, NY:] = im
-
+            target[k, rows, :NY] = re
+            target[k, rows, NY:] = im
+
+
+def boltzmann(slot, wi_ref, tz, work, total_ref, sum_ref):
     for k in range(KX):
         re, im = z_stage(tz, work[k], 1.0)
         work[k, :, :NY] = re
@@ -355,9 +358,12 @@
 
 def energy_kernel(
     slabs,
+    probes,
+    cells,
     ids,
     rots,
     offs,
+    weights,
     turns,
     receptor,
     library,
@@ -369,8 +375,7 @@
     tz_ref,
     wf_ref,
     wi_ref,
-    total_ref,
-    sum_ref,
+    out_ref,
     lib,
     te,
     to,
@@ -387,25 +392,47 @@
     q,
     spec,
     work,
+    joint,
+    total,
+    sums,
+    mine,
+    gathered,
+    faces,
+    mixed,
+    blocks,
     send,
     recv,
     hand_send,
     hand_recv,
     near,
+    part_send,
+    part_recv,
+    face_send,
+    face_recv,
+    block_send,
+    block_recv,
 ):
-    terms = receptor.shape[0]
+    terms, planes = receptor.shape[0], receptor.shape[1]
     half = terms // 2
-    slots = total_ref.shape[0]
+    slots = total.shape[0]
+    rows = out_ref.shape[1]
     slab = lax.axis_index("slab")
     probe = lax.axis_index("probe")
     core = lax.rem(probe, 2)
     right = {"slab": lax.rem(slab + 1, slabs)}
     left = {"slab": lax.rem(slab + slabs - 1, slabs)}
-    other = {"probe": probe + 1 - 2 * core}
+    sibling = probe + 1 - 2 * core
+    partner = lax.rem(probe + 2, probes)
+    other = {"probe": sibling}
 
     barrier = pltpu.get_barrier_semaphore()
-    for device in (left, right, other):
-        pl.semaphore_signal(barrier, inc=1, device_id=device, device_id_type=MESH)
+
+    @pl.loop(1, slabs)
+    def _(d):
+        pl.semaphore_signal(barrier, inc=1, device_id={"slab": lax.rem(slab + d, slabs)}, device_id_type=MESH)
+
+    for device in (sibling, partner):
+        pl.semaphore_signal(barrier, inc=1, device_id={"probe": device}, device_id_type=MESH)
     nearby = [
         pltpu.make_async_copy(library, lib, near.at[0]),
         pltpu.make_async_copy(te_hbm, te, near.at[1]),
@@ -413,7 +440,7 @@
         pltpu.make_async_copy(receptor.at[pl.ds(core * half, half)], own.at[pl.ds(0, half)], near.at[3]),
         pltpu.make_async_copy(receptor.at[pl.ds((1 - core) * half, half)], own.at[pl.ds(half, half)], near.at[4]),
     ]
-    pl.semaphore_wait(barrier, 3)
+    pl.semaphore_wait(barrier, slabs - 1 + 2)
 
     def halo_copy(j, side):
         return pltpu.make_async_remote_copy(
@@ -456,18 +483,9 @@
         def _(p):
             probe_pair(p, te, to, even, odd, tzs, ph, q)
 
-    pairs(0, 3)
-    hand_over(0)
-    pairs(3, PAIRS)
-    hand_over(1)
     tz = tz_ref[...]
 
-    @pl.loop(0, half)
-    def _(j):
-        @pl.when(j >= 2)
-        def _():
-            hand_over(j)
-
+    def transforms(j):
         @pl.loop(0, 2)
         def _(h):
             @pl.when(h == 1)
@@ -477,76 +495,53 @@
 
             forward(j + half * h, own, before, after, wf_ref, tz, work, spec)
 
+    pairs(0, 3)
+    hand_over(0)
+    pairs(3, PAIRS)
+    hand_over(1)
+
+    @pl.loop(0, 2)
+    def _(j):
+        transforms(j)
+
     @pl.loop(0, slots)
     def _(slot):
-        boltzmann(slot, q, wi_ref, tz, work, spec, total_ref, sum_ref)
-
-    @pl.loop(0, half)
-    def _(j):
+        contract(slot, (0, 1, half, half + 1), q, spec, None, joint.at[slot])
+
+    hand_over(2)
+    transforms(2)
+
+    @pl.loop(0, slots)
+    def _(slot):
+        contract(slot, (2, half + 2), q, spec, joint.at[slot], joint.at[slot])
+
+    hand_over(3)
+    transforms(3)
+
+    def face_copy(slot, side):
+        return pltpu.make_async_remote_copy(
+            src_ref=total.at[slot, (planes - 1, 0)[side]],
+            dst_ref=faces.at[side, slot],
+            send_sem=face_send.at[side, slot],
+            recv_sem=face_recv.at[side, slot],
+            device_id=(right, left)[side],
+            device_id_type=MESH,
+        )
+
+    @pl.loop(0, slots)
+    def _(slot):
+        contract(slot, (3, half + 3), q, spec, joint.at[slot], work)
+        boltzmann(slot, wi_ref, tz, work, total, sums)
         for side in range(2):
-            halo_copy(j, side).wait_send()
-            hand_copy(j, side).wait_send()
-
-
-def sum_terms(terms):
-    total = None
-    for coef, value in terms:
-        if abs(coef) < 1e-15:
-            continue
-        total = coef * value if total is None else total + coef * value
-    return total
-
-
-def tail_kernel(
-    slabs,
-    probes,
-    cells,
-    types,
-    total_ref,
-    sum_ref,
-    weight_ref,
-    out_ref,
-    mine,
-    gathered,
-    halo,
-    mixed,
-    blocks,
-    part_send,
-    part_recv,
-    halo_send,
-    halo_recv,
-    block_send,
-    block_recv,
-):
-    slots = total_ref.shape[0]
-    planes = total_ref.shape[1]
-    rows = out_ref.shape[1]
-    slab = lax.axis_index("slab")
-    probe = lax.axis_index("probe")
-
-    barrier = pltpu.get_barrier_semaphore()
-
-    @pl.loop(1, slabs)
-    def _(d):
-        pl.semaphore_signal(
-            barrier, inc=1, device_id={"slab": lax.rem(slab + d, slabs)}, device_id_type=MESH
-        )
-
-    for d in range(1, probes):
-        pl.semaphore_signal(
-            barrier, inc=1, device_id={"probe": lax.rem(probe + d, probes)}, device_id_type=MESH
-        )
+            face_copy(slot, side).start()
 
     parts = []
     for s in range(slots):
-        v = jnp.sum(sum_ref[s], axis=0, keepdims=True)
-        v = jnp.sum(v, axis=1, keepdims=True)
-        parts.append(jnp.broadcast_to(v, (1, NY)))
+        v = jnp.sum(sums[s], axis=0, keepdims=True)
+        parts.append(jnp.broadcast_to(jnp.sum(v, axis=1, keepdims=True), (1, NY)))
     parts += [jnp.zeros((1, NY), F32)] * (8 - slots)
-    own = jnp.concatenate(parts, axis=0)
-    mine[...] = own
-
-    pl.semaphore_wait(barrier, slabs - 1 + probes - 1)
+    local_part = jnp.concatenate(parts, axis=0)
+    mine[...] = local_part
 
     def part_copy(d):
         return pltpu.make_async_remote_copy(
@@ -562,99 +557,116 @@
     def _(d):
         part_copy(d).start()
 
-    to_right = pltpu.make_async_remote_copy(
-        src_ref=total_ref.at[:, planes - 1],
-        dst_ref=halo.at[0],
-        send_sem=halo_send.at[0],
-        recv_sem=halo_recv.at[0],
-        device_id={"slab": lax.rem(slab + 1, slabs)},
-        device_id_type=MESH,
-    )
-    to_left = pltpu.make_async_remote_copy(
-        src_ref=total_ref.at[:, 0],
-        dst_ref=halo.at[1],
-        send_sem=halo_send.at[1],
-        recv_sem=halo_recv.at[1],
-        device_id={"slab": lax.rem(slab + slabs - 1, slabs)},
-        device_id_type=MESH,
-    )
-    to_right.start()
-    to_left.start()
+    @pl.loop(0, slots)
+    def _(slot):
+        for side in range(2):
+            face_copy(slot, side).wait_recv()
 
     @pl.loop(1, slabs)
     def _(d):
         part_copy(d).wait_recv()
 
-    partition = own
+    partition = local_part
     for d in range(1, slabs):
         partition = partition + gathered[d]
-    coef = weight_ref[...] * (cells / partition)
-    coefs = [jnp.broadcast_to(coef[s : s + 1], (8, NY)) for s in range(slots)]
+    share = cells / partition
+    coefs = [jnp.broadcast_to(share[s : s + 1] * weights[ids[s]], (8, NY)) for s in range(slots)]
 
     def weighted(read):
-        total = None
+        result = None
         for s in range(slots):
             v = read(s).reshape(NZ // 8, 8, NY) * coefs[s][None]
-            total = v if total is None else total + v
-        return total.reshape(NZ, NY)
-
-    to_right.wait_recv()
-    to_left.wait_recv()
-    mixed[0] = weighted(lambda s: halo[0, s])
-    mixed[planes + 1] = weighted(lambda s: halo[1, s])
+            result = v if result is None else result + v
+        return result.reshape(NZ, NY)
+
+    mixed[0] = weighted(lambda s: faces[0, s])
+    mixed[planes + 1] = weighted(lambda s: faces[1, s])
     for x in range(planes):
-        mixed[x + 1] = weighted(lambda s: total_ref[s, x])
+        mixed[x + 1] = weighted(lambda s: total[s, x])
     for x in range(planes):
         v = (mixed[x] + 2.0 * mixed[x + 1] + mixed[x + 2]) * 0.25
         v = (pltpu.roll(v, 1, 0) + 2.0 * v + pltpu.roll(v, NZ - 1, 0)) * 0.25
         v = (pltpu.roll(v, 1, 1) + 2.0 * v + pltpu.roll(v, NY - 1, 1)) * 0.25
         mixed[x] = v
 
-    def block_copy(d):
-        target = lax.rem(probe + d, probes)
-        return pltpu.make_async_remote_copy(
-            src_ref=mixed.at[pl.ds(0, planes), pl.ds(pl.multiple_of(target * rows, 8), rows)],
-            dst_ref=blocks.at[d - 1],
-            send_sem=block_send.at[d - 1],
-            recv_sem=block_recv.at[d - 1],
-            device_id={"probe": target},
+    def block(p):
+        return mixed.at[pl.ds(0, planes), pl.ds(pl.multiple_of(p * rows, 8), rows)]
+
+    away = partner + sibling - probe
+    crossing = [
+        pltpu.make_async_remote_copy(
+            src_ref=block(p),
+            dst_ref=blocks.at[i],
+            send_sem=block_send.at[i],
+            recv_sem=block_recv.at[i],
+            device_id={"probe": device},
             device_id_type=MESH,
         )
-
-    for d in range(1, probes):
-        block_copy(d).start()
-    result = mixed[pl.ds(0, planes), pl.ds(pl.multiple_of(probe * rows, 8), rows)]
-    for d in range(1, probes):
-        block_copy(d).wait_recv()
-        result = result + blocks[d - 1]
-    out_ref[...] = result * (1.0 / types)
+        for i, (p, device) in enumerate(((away, sibling), (sibling, sibling)))
+    ]
+    last = pltpu.make_async_remote_copy(
+        src_ref=blocks.at[2],
+        dst_ref=blocks.at[3],
+        send_sem=block_send.at[2],
+        recv_sem=block_recv.at[2],
+        device_id={"probe": partner},
+        device_id_type=MESH,
+    )
+    for copy in crossing:
+        copy.start()
+    crossing[0].wait_recv()
+    blocks[2] = block(partner)[...] + blocks[0]
+    last.start()
+    crossing[1].wait_recv()
+    result = block(probe)[...] + blocks[1]
+    last.wait_recv()
+    out_ref[...] = (result + blocks[3]) * (1.0 / weights.shape[0])
+
+    @pl.loop(0, half)
+    def _(j):
+        for side in range(2):
+            halo_copy(j, side).wait_send()
+            hand_copy(j, side).wait_send()
+
+    @pl.loop(0, slots)
+    def _(slot):
+        for side in range(2):
+            face_copy(slot, side).wait_send()
 
     @pl.loop(1, slabs)
     def _(d):
         part_copy(d).wait_send()
 
-    to_right.wait_send()
-    to_left.wait_send()
-    for d in range(1, probes):
-        block_copy(d).wait_send()
-
-
-def energy_call(slabs, receptor, library, probe_ids, rotations, offsets):
+    for copy in (*crossing, last):
+        copy.wait_send()
+
+
+def sum_terms(terms):
+    total = None
+    for coef, value in terms:
+        if abs(coef) < 1e-15:
+            continue
+        total = coef * value if total is None else total + coef * value
+    return total
+
+
+def local(receptor, library, probe_ids, rotations, offsets, probe_weight):
     terms, planes, nz, ny = receptor.shape
+    slabs = lax.axis_size("slab")
+    probes = lax.axis_size("probe")
     slots, half = probe_ids.shape[0], terms // 2
+    rows = nz // probes
+    cells = float(planes * slabs * nz * ny)
     te, to = xy_tables()
     smem = pl.BlockSpec(memory_space=pltpu.SMEM)
     vmem = pl.BlockSpec(memory_space=pltpu.VMEM)
     hbm = pl.BlockSpec(memory_space=pl.ANY)
     dma = pltpu.SemaphoreType.DMA
     return pl.pallas_call(
-        functools.partial(energy_kernel, slabs),
-        in_specs=[smem] * 4 + [hbm] * 4 + [vmem] * 6,
-        out_specs=[vmem, vmem],
-        out_shape=[
-            jax.ShapeDtypeStruct((slots, planes, nz, ny), F32),
-            jax.ShapeDtypeStruct((slots, 8, ny), F32),
-        ],
+        functools.partial(energy_kernel, slabs, probes, cells),
+        in_specs=[smem] * 5 + [hbm] * 4 + [vmem] * 6,
+        out_specs=vmem,
+        out_shape=jax.ShapeDtypeStruct((planes, rows, ny), F32),
         scratch_shapes=[
             pltpu.VMEM(library.shape, F32),
             pltpu.VMEM(te.shape, BF),
@@ -672,20 +684,35 @@
             pltpu.VMEM((slots, terms, PAIRS, 2 * NZ, 2 * NY), F32),
             pltpu.VMEM((terms, KX, nz, 2 * ny), F32),
             pltpu.VMEM((KX, nz, 2 * ny), F32),
+            pltpu.VMEM((slots, KX, nz, 2 * ny), F32),
+            pltpu.VMEM((slots, planes, nz, ny), F32),
+            pltpu.VMEM((slots, 8, ny), F32),
+            pltpu.VMEM((8, ny), F32),
+            pltpu.VMEM((slabs, 8, ny), F32),
+            pltpu.VMEM((2, slots, nz, ny), F32),
+            pltpu.VMEM((planes + 2, nz, ny), F32),
+            pltpu.VMEM((4, planes, rows, ny), F32),
             dma((2, half)),
             dma((2, half)),
             dma((2, half)),
             dma((2, half)),
             dma((5,)),
+            dma((slabs,)),
+            dma((slabs,)),
+            dma((2, slots)),
+            dma((2, slots)),
+            dma((3,)),
+            dma((3,)),
         ],
         compiler_params=pltpu.CompilerParams(
-            collective_id=1, has_side_effects=True, vmem_limit_bytes=63 << 20
+            collective_id=0, has_side_effects=True, vmem_limit_bytes=63 << 20
         ),
-        name="energy_maps",
+        name="consensus_density",
     )(
         probe_ids,
         rotations,
         offsets,
+        probe_weight,
         jnp.asarray(rotation_table()),
         receptor,
         library,
@@ -700,48 +727,6 @@
     )
 
 
-def local(receptor, library, probe_ids, rotations, offsets, probe_weight):
-    terms, planes, nz, ny = receptor.shape
-    slabs = lax.axis_size("slab")
-    probes = lax.axis_size("probe")
-    slots = probe_ids.shape[0]
-    types = probe_weight.shape[0]
-    cells = float(planes * slabs * nz * ny)
-
-    total, sums = energy_call(
-        slabs, receptor, library, probe_ids, rotations.reshape(-1), offsets.reshape(-1)
-    )
-
-    onehot = (probe_ids[:, None] == jnp.arange(types, dtype=jnp.int32)[None, :]).astype(F32)
-    chosen = jnp.sum(onehot * probe_weight[None], axis=1)
-    weight = jnp.broadcast_to(jnp.pad(chosen, (0, 8 - slots))[:, None], (8, ny))
-    rows = nz // probes
-    vmem = pl.BlockSpec(memory_space=pltpu.VMEM)
-    return pl.pallas_call(
-        functools.partial(tail_kernel, slabs, probes, cells, types),
-        in_specs=[vmem] * 3,
-        out_specs=vmem,
-        out_shape=jax.ShapeDtypeStruct((planes, rows, ny), F32),
-        scratch_shapes=[
-            pltpu.VMEM((8, ny), F32),
-            pltpu.VMEM((slabs, 8, ny), F32),
-            pltpu.VMEM((2, slots, nz, ny), F32),
-            pltpu.VMEM((planes + 2, nz, ny), F32),
-            pltpu.VMEM((probes - 1, planes, rows, ny), F32),
-            pltpu.SemaphoreType.DMA((slabs,)),
-            pltpu.SemaphoreType.DMA((slabs,)),
-            pltpu.SemaphoreType.DMA((2,)),
-            pltpu.SemaphoreType.DMA((2,)),
-            pltpu.SemaphoreType.DMA((probes - 1,)),
-            pltpu.SemaphoreType.DMA((probes - 1,)),
-        ],
-        compiler_params=pltpu.CompilerParams(
-            collective_id=0, has_side_effects=True, vmem_limit_bytes=24 << 20
-        ),
-        name="consensus_tail",
-    )(total, sums, weight)
-
-
 def solution(mesh):
     in_specs = (
         P(None, "slab", None, None),

time: 74.2 us -> 67.1 us (0.904)
  Pallas kernels: 69.1 us -> 62.8 us
  other arithmetic: 0.85 us -> 0 us
    pallas_call x2 -> x1, Pallas kernels: 69.1 us -> 62.8 us  [local(): pl.pallas_call(functools.partial(energy_kernel, slabs, probes, cells), in...]
    reduce_sum x1 -> x0, other arithmetic: 0.85 us -> none  [local(): chosen = jnp.sum(onehot * probe_weight[None], axis=1)]
    unnamed x6 -> x3, local copies, waits for them, and re-layouts: 3.33 us -> 4.11 us
where the time goes in v4:
time: 67.1 us; the launch traced here: 66.9 us
  Pallas kernels  62.8 us (94%)
  local copies, waits for them, and re-layouts  4.11 us (6%)
    pallas_call x1, Pallas kernels, local(): pl.pallas_call(functools.partial(energy_kernel, slabs, probes, cells), in...  62.8 us
    unnamed x3, local copies, waits for them, and re-layouts  4.11 us

profile of v4, /device:TPU:1, one launch (start us, length us, event | category | flops | bytes accessed | tf_op | source)
XLA Modules:
  0.0 66.9 jit_solution(9090092819816462592)
XLA Ops:
  0.0 1.3 %copy.16.rots = s32[4,1]{1,0:T(4,128)} copy(s32[4,1]{0,1:T(1,128)} %param.18) | data formatting | bytes 32 | tf_op args[3]
  1.3 1.3 %copy.17.offs = s32[4,1,2]{2,1,0:T(1,128)} copy(s32[4,1,2]{0,2,1:T(2,128)} %param.19) | data formatting | bytes 64 | tf_op args[4]
  2.6 62.8 %consensus_density.1 = f32[8,16,128]{2,1,0:T(8,128)} custom-call(s32[4]{0:T(128)} %ids.1, s32[4,1]{1,0:T(4,128)} %copy.16.rots, s32[4,1,2]{2,1,0:T(1,128)} %copy.17.offs, f32[16]{0:T(128)} %weights.1, s32[24,4]{1,0:T(8,128)} %constant.18.clone.turns, f32[8,8,64,128]{3,2,1,0:T(8,128)} %receptor.1, f32[16,8,4913]{2,1,0:T(8,128)} %library.1, ...), custom_call_target="tpu_custom_call" | custom-call | tf_op jit(solution)/shard_map/consensus_density/pallas_call | solution.py:665
  65.4 1.5 %copy.19 = f32[8,16,128]{2,1,0:T(8,128)} copy(f32[8,16,128]{2,1,0:T(8,128)} %consensus_density.1) | data formatting | bytes 131072

commit v5 on v4

--- a/solution.py
+++ b/solution.py
@@ -74,12 +74,14 @@
 
 def lane_offsets():
     ax, ay = half_offsets()
-    rows = np.full((8, PACK), 10000, np.int32)
-    for c in range(3):
-        rows[0, c * HALF : (c + 1) * HALF] = ax
-        rows[1, c * HALF : (c + 1) * HALF] = ay
-    rows[2] = 0
-    rows[2, [0, HALF, 2 * HALF]] = 10000
+    rows = np.full((8, CUBE), 10000, np.int32)
+    rows[2:] = 0
+    for c in range(2):
+        lanes = slice(c * HALF, (c + 1) * HALF)
+        rows[0, lanes] = ax
+        rows[1, lanes] = ay
+        rows[2, c * HALF] = 10000
+        rows[3, lanes] = 1 - 2 * c
     return rows
 
 
@@ -136,13 +138,10 @@
     return hi, lo
 
 
-def turned_probes(ids, rots, offs, turns, core, lib_ref, swap_ref, lane_ref, zstep_ref, xa, xb, kd, even, odd, tzs, ph):
-    slots, terms = tzs.shape[0], lib_ref.shape[1]
-    xa[...] = jnp.zeros_like(xa)
-    kd[...] = jnp.zeros_like(kd)
+def turned_probes(first, last, ids, rots, offs, turns, core, lib_ref, swap_ref, lane_ref, zstep_ref, xa, xb, kd, even, odd, tzs, ph):
+    terms = lib_ref.shape[1]
     lane = lax.broadcasted_iota(jnp.int32, (terms, CUBE), 1)
-    packed_lane = lax.broadcasted_iota(jnp.int32, (terms * AZ, 128), 1)
-    source = lax.broadcasted_iota(jnp.int32, (CUBE, PACK), 0)
+    source = lax.broadcasted_iota(jnp.int32, (CUBE, CUBE), 0)
     zlane = lax.broadcasted_iota(jnp.int32, (2 * NZ, 6 * AZ), 1)
     ky = lax.broadcasted_iota(jnp.int32, (8, 2 * NY), 1) % NY
 
@@ -151,12 +150,12 @@
         out = jnp.dot(jnp.concatenate([hi, lo], axis=0), table, preferred_element_type=F32)
         return out[: x.shape[0]] + out[x.shape[0] :]
 
-    @pl.loop(0, slots)
+    @pl.loop(first, last)
     def _(slot):
-        rot = rots[slot, 0]
+        rot = rots[slot]
         zaxis, flipped = turns[rot, 0], turns[rot, 1]
         step_x, step_y = turns[rot, 2], turns[rot, 3]
-        off_y, off_z = offs[slot, 0, 0], offs[slot, 0, 1]
+        off_y, off_z = offs[2 * slot], offs[2 * slot + 1]
 
         turn = (zstep_ref[0] - zstep_ref[1] * off_z + NZ * NZ) & (NZ - 1)
         t = jnp.cos(turn.astype(F32) * (2 * math.pi / NZ)) * zstep_ref[2].astype(F32)
@@ -173,30 +172,29 @@
         swapped = permuted(x.reshape(KS * terms, CUBE), swap_ref[...]).reshape(KS, terms, CUBE)
         xa[...] = jnp.where(zaxis == 2, swapped, x)
         for m in range(KS):
-            acc = jnp.zeros((terms, CUBE), F32)
-            for n in range(KS):
-                moved = pltpu.roll(xa[n], ((n - m) * KS) % CUBE, 1)
-                acc = jnp.where((lane >= n * KS) & (lane < (n + 1) * KS), moved, acc)
+            acc = jnp.concatenate(
+                [xa[n, :, m * KS : (m + 1) * KS] for n in range(KS)] + [jnp.zeros((terms, CUBE - KS * KS), F32)],
+                axis=1,
+            )
             xb[m] = jnp.where(zaxis == 0, xa[m], acc)
 
         here = lane_ref[0:1] * step_x + lane_ref[1:2] * step_y + (HALF - 1)
         there = 2 * (HALF - 1) - here + lane_ref[2:3]
         plus = (source == here).astype(F32)
-        minus = (source == there).astype(F32)
-        x = xb[...].reshape(KS * terms, CUBE)
-        for table, ref in ((plus + minus, even), (plus - minus, odd)):
-            turned = permuted(x, table.astype(BF))
-            for m in range(KS):
-                f = KS - 1 - m
-                row = jnp.where(flipped == 1, turned[f * terms : (f + 1) * terms], turned[m * terms : (m + 1) * terms])
-                for j in range(PACK // 128):
-                    kd[j, pl.ds(m, terms, stride=AZ), :] = row[:, j * 128 : (j + 1) * 128]
-            rows = pl.ds(pl.multiple_of(slot * terms * AZ, terms * AZ), terms * AZ)
-            for j in range(PACK // 128):
-                hi, lo = split(kd[j])
-                packed = packed_lane + j * 128
-                low = (packed >= HALF) & (packed < 2 * HALF)
-                ref[rows, j * 128 : (j + 1) * 128] = jnp.where(low, lo.astype(F32), hi.astype(F32)).astype(BF)
+        minus = jnp.where(source == there, lane_ref[3:4], 0).astype(F32)
+        turned = permuted(xb[...].reshape(KS * terms, CUBE), (plus + minus).astype(BF))
+        for m in range(KS):
+            f = KS - 1 - m
+            row = jnp.where(flipped == 1, turned[f * terms : (f + 1) * terms], turned[m * terms : (m + 1) * terms])
+            for j in range(CUBE // 128):
+                kd[j, pl.ds(m, terms, stride=AZ), :] = row[:, j * 128 : (j + 1) * 128]
+        rows = pl.ds(pl.multiple_of(slot * terms * AZ, terms * AZ), terms * AZ)
+        both = jnp.concatenate([kd[j] for j in range(CUBE // 128)], axis=1)
+        hi, lo = split(both)
+        hi, lo = hi.astype(F32), lo.astype(F32)
+        spare = jnp.zeros((terms * AZ, PACK - 3 * HALF), F32)
+        for ref, lanes in ((even, slice(0, HALF)), (odd, slice(HALF, 2 * HALF))):
+            ref[rows, :] = jnp.concatenate([hi[:, lanes], lo[:, lanes], hi[:, lanes], spare], axis=1).astype(BF)
 
 
 def probe_pair(p, te, to, even, odd, tzs, ph, q):
@@ -282,7 +280,7 @@
 
 
 def forward(i, own, before, after, wf_ref, tz, work, spec):
-    @pl.loop(0, 8)
+    @pl.loop(0, 8, unroll=True)
     def _(chunk):
         rows = pl.ds(pl.multiple_of(chunk * 8, 8), 8)
         r = (
@@ -304,7 +302,7 @@
 
 
 def contract(slot, group, q, spec, source, target):
-    @pl.loop(0, 8)
+    @pl.loop(0, 8, unroll=2)
     def _(chunk):
         start = pl.multiple_of(chunk * 8, 8)
         rows = pl.ds(start, 8)
@@ -335,7 +333,7 @@
     sum_ref[slot] = jnp.zeros((8, NY), F32)
     scale = 1.0 / (EXT * NZ * NY)
 
-    @pl.loop(0, 8)
+    @pl.loop(0, 8, unroll=4)
     def _(chunk):
         rows = pl.ds(pl.multiple_of(chunk * 8, 8), 8)
         fr = [work[k, rows, :NY] for k in range(KX)]
@@ -440,7 +438,6 @@
         pltpu.make_async_copy(receptor.at[pl.ds(core * half, half)], own.at[pl.ds(0, half)], near.at[3]),
         pltpu.make_async_copy(receptor.at[pl.ds((1 - core) * half, half)], own.at[pl.ds(half, half)], near.at[4]),
     ]
-    pl.semaphore_wait(barrier, slabs - 1 + 2)
 
     def halo_copy(j, side):
         return pltpu.make_async_remote_copy(
@@ -468,15 +465,34 @@
             halo_copy(j, side).wait_recv()
             hand_copy(j, side).start()
 
-    for j in range(half):
+    for copy in nearby:
+        copy.start()
+    xa[...] = jnp.zeros_like(xa)
+    kd[...] = jnp.zeros_like(kd)
+    pl.semaphore_wait(barrier, slabs - 1 + 2)
+
+    def send_off(j):
         for side in range(2):
             halo_copy(j, side).start()
-    for copy in nearby:
-        copy.start()
+
+    send_off(0)
     nearby[0].wait()
-    turned_probes(ids, rots, offs, turns, core, lib, swap_ref, lane_ref, zstep_ref, xa, xb, kd, even, odd, tzs, ph)
+    early = slots - 1
+
+    @pl.loop(0, 2)
+    def _(part):
+        turned_probes(
+            part * early, early + part * (slots - early),
+            ids, rots, offs, turns, core, lib, swap_ref, lane_ref, zstep_ref, xa, xb, kd, even, odd, tzs, ph,
+        )
+
+        @pl.when(part == 0)
+        def _():
+            send_off(1)
+
     for copy in nearby[1:]:
         copy.wait()
+    hand_over(0)
 
     def pairs(low, high):
         @pl.loop(low, high)
@@ -485,38 +501,41 @@
 
     tz = tz_ref[...]
 
-    def transforms(j):
-        @pl.loop(0, 2)
-        def _(h):
-            @pl.when(h == 1)
-            def _():
-                for side in range(2):
-                    hand_copy(j, side).wait_recv()
-
-            forward(j + half * h, own, before, after, wf_ref, tz, work, spec)
+    def products(group, first):
+        @pl.loop(0, slots)
+        def _(slot):
+            contract(slot, group, q, spec, None if first else joint.at[slot], joint.at[slot])
 
     pairs(0, 3)
-    hand_over(0)
-    pairs(3, PAIRS)
+    send_off(2)
+    pairs(3, 5)
     hand_over(1)
-
-    @pl.loop(0, 2)
-    def _(j):
-        transforms(j)
-
-    @pl.loop(0, slots)
-    def _(slot):
-        contract(slot, (0, 1, half, half + 1), q, spec, None, joint.at[slot])
-
-    hand_over(2)
-    transforms(2)
-
-    @pl.loop(0, slots)
-    def _(slot):
-        contract(slot, (2, half + 2), q, spec, joint.at[slot], joint.at[slot])
-
-    hand_over(3)
-    transforms(3)
+    pairs(5, PAIRS)
+    send_off(3)
+
+    @pl.loop(0, terms)
+    def _(i):
+        j, h = i // 2, i % 2
+
+        @pl.when(h == 1)
+        def _():
+            for side in range(2):
+                hand_copy(j, side).wait_recv()
+
+        forward(j + half * h, own, before, after, wf_ref, tz, work, spec)
+
+        @pl.when(i == 1)
+        def _():
+            hand_over(2)
+
+        @pl.when(i == 3)
+        def _():
+            products((0, 1, half, half + 1), True)
+            hand_over(3)
+
+        @pl.when(i == 5)
+        def _():
+            products((2, half + 2), False)
 
     def face_copy(slot, side):
         return pltpu.make_async_remote_copy(
@@ -676,7 +695,7 @@
             pltpu.VMEM(receptor.shape, F32),
             pltpu.VMEM((KS, terms, CUBE), F32),
             pltpu.VMEM((KS, terms, CUBE), F32),
-            pltpu.VMEM((PACK // 128, terms * AZ, 128), F32),
+            pltpu.VMEM((CUBE // 128, terms * AZ, 128), F32),
             pltpu.VMEM((slots * terms * AZ, PACK), BF),
             pltpu.VMEM((slots * terms * AZ, PACK), BF),
             pltpu.VMEM((slots, 2 * NZ, 6 * AZ), BF),
@@ -710,8 +729,8 @@
         name="consensus_density",
     )(
         probe_ids,
-        rotations,
-        offsets,
+        rotations.reshape(-1),
+        offsets.reshape(-1),
         probe_weight,
         jnp.asarray(rotation_table()),
         receptor,

time: 67.1 us -> 64.6 us (0.963)
  Pallas kernels: 62.8 us -> 61.5 us
  local copies, waits for them, and re-layouts: 4.11 us -> 2.83 us
    unnamed x3 -> x2, local copies, waits for them, and re-layouts: 4.11 us -> 2.24 us
    pallas_call x1, Pallas kernels: 62.8 us -> 61.5 us  [local(): pl.pallas_call(functools.partial(energy_kernel, slabs, probes, cells), in...]
where the time goes in v5:
time: 64.6 us; the launch traced here: 64.4 us
  Pallas kernels  61.5 us (95%)
  local copies, waits for them, and re-layouts  2.83 us (4%)
    pallas_call x1, Pallas kernels, local(): pl.pallas_call(functools.partial(energy_kernel, slabs, probes, cells), in...  61.5 us
    unnamed x2, local copies, waits for them, and re-layouts  2.24 us

profile of v5, /device:TPU:1, one launch (start us, length us, event | category | flops | bytes accessed | tf_op | source)
XLA Modules:
  0.0 64.4 jit_solution(10822700854317222406)
XLA Ops:
  0.0 0.8 %copy.17 = s32[4,1,2]{2,0,1:T(4,128)S(1)} copy(s32[4,1,2]{0,2,1:T(2,128)} %param.19) | data formatting | bytes 64 | tf_op args[4]
  0.8 0.6 reshape.7.offs
  1.4 61.5 %consensus_density.1 = f32[8,16,128]{2,1,0:T(8,128)} custom-call(s32[4]{0:T(128)} %ids.1, s32[4]{0:T(128)} %bitcast.3, s32[8]{0:T(128)} %reshape.7.offs, f32[16]{0:T(128)} %weights.1, s32[24,4]{1,0:T(8,128)} %constant.18.clone.turns, f32[8,8,64,128]{3,2,1,0:T(8,128)} %receptor.1, f32[16,8,4913]{2,1,0:T(8,128)} %library.1, ...), custom_call_target="tpu_custom_call" | custom-call | tf_op jit(solution)/shard_map/consensus_density/pallas_call | solution.py:684
  62.9 1.5 %copy.19 = f32[8,16,128]{2,1,0:T(8,128)} copy(f32[8,16,128]{2,1,0:T(8,128)} %consensus_density.1) | data formatting | bytes 131072

commit v6 on v5

--- a/solution.py
+++ b/solution.py
@@ -566,8 +566,8 @@
         return pltpu.make_async_remote_copy(
             src_ref=mine,
             dst_ref=gathered.at[d],
-            send_sem=part_send.at[d],
-            recv_sem=part_recv.at[d],
+            send_sem=part_send,
+            recv_sem=part_recv,
             device_id={"slab": lax.rem(slab + d, slabs)},
             device_id_type=MESH,
         )
@@ -581,9 +581,8 @@
         for side in range(2):
             face_copy(slot, side).wait_recv()
 
-    @pl.loop(1, slabs)
-    def _(d):
-        part_copy(d).wait_recv()
+    others = gathered.at[pl.ds(1, slabs - 1)]
+    pltpu.make_async_copy(others, others, part_recv).wait()
 
     partition = local_part
     for d in range(1, slabs):
@@ -652,9 +651,7 @@
         for side in range(2):
             face_copy(slot, side).wait_send()
 
-    @pl.loop(1, slabs)
-    def _(d):
-        part_copy(d).wait_send()
+    pltpu.make_async_copy(others, others, part_send).wait()
 
     for copy in (*crossing, last):
         copy.wait_send()
@@ -716,8 +713,8 @@
             dma((2, half)),
             dma((2, half)),
             dma((5,)),
-            dma((slabs,)),
-            dma((slabs,)),
+            pltpu.SemaphoreType.DMA,
+            pltpu.SemaphoreType.DMA,
             dma((2, slots)),
             dma((2, slots)),
             dma((3,)),

time: 64.6 us -> 63.6 us (0.985)
  Pallas kernels: 61.5 us -> 60.6 us
    pallas_call x1, Pallas kernels: 61.5 us -> 60.6 us  [local(): pl.pallas_call(functools.partial(energy_kernel, slabs, probes, cells), in...]
where the time goes in v6:
time: 63.6 us; the launch traced here: 63.4 us
  Pallas kernels  60.6 us (95%)
  local copies, waits for them, and re-layouts  2.83 us (4%)
    pallas_call x1, Pallas kernels, local(): pl.pallas_call(functools.partial(energy_kernel, slabs, probes, cells), in...  60.6 us
    unnamed x2, local copies, waits for them, and re-layouts  2.24 us

profile of v6, /device:TPU:1, one launch (start us, length us, event | category | flops | bytes accessed | tf_op | source)
XLA Modules:
  0.0 63.4 jit_solution(11718366333794289834)
XLA Ops:
  0.0 0.8 %copy.17 = s32[4,1,2]{2,0,1:T(4,128)S(1)} copy(s32[4,1,2]{0,2,1:T(2,128)} %param.19) | data formatting | bytes 64 | tf_op args[4]
  0.8 0.6 reshape.7.offs
  1.4 60.6 %consensus_density.1 = f32[8,16,128]{2,1,0:T(8,128)} custom-call(s32[4]{0:T(128)} %ids.1, s32[4]{0:T(128)} %bitcast.3, s32[8]{0:T(128)} %reshape.7.offs, f32[16]{0:T(128)} %weights.1, s32[24,4]{1,0:T(8,128)} %constant.18.clone.turns, f32[8,8,64,128]{3,2,1,0:T(8,128)} %receptor.1, f32[16,8,4913]{2,1,0:T(8,128)} %library.1, ...), custom_call_target="tpu_custom_call" | custom-call | tf_op jit(solution)/shard_map/consensus_density/pallas_call | solution.py:681
  62.0 1.5 %copy.19 = f32[8,16,128]{2,1,0:T(8,128)} copy(f32[8,16,128]{2,1,0:T(8,128)} %consensus_density.1) | data formatting | bytes 131072

commit v7 on v6

--- a/solution.py
+++ b/solution.py
@@ -302,7 +302,7 @@
 
 
 def contract(slot, group, q, spec, source, target):
-    @pl.loop(0, 8, unroll=2)
+    @pl.loop(0, 8, unroll=4)
     def _(chunk):
         start = pl.multiple_of(chunk * 8, 8)
         rows = pl.ds(start, 8)

time: 63.6 us -> 63.7 us (level)
  no operation moved by 1% of the time
where the time goes in v7:
time: 63.7 us; the launch traced here: 63.5 us
  Pallas kernels  60.6 us (95%)
  local copies, waits for them, and re-layouts  2.83 us (4%)
    pallas_call x1, Pallas kernels, local(): pl.pallas_call(functools.partial(energy_kernel, slabs, probes, cells), in...  60.6 us
    unnamed x2, local copies, waits for them, and re-layouts  2.24 us

profile of v7, /device:TPU:1, one launch (start us, length us, event | category | flops | bytes accessed | tf_op | source)
XLA Modules:
  0.0 63.5 jit_solution(16276791457660991780)
XLA Ops:
  0.0 0.8 %copy.17 = s32[4,1,2]{2,0,1:T(4,128)S(1)} copy(s32[4,1,2]{0,2,1:T(2,128)} %param.19) | data formatting | bytes 64 | tf_op args[4]
  0.8 0.6 reshape.7.offs
  1.4 60.6 %consensus_density.1 = f32[8,16,128]{2,1,0:T(8,128)} custom-call(s32[4]{0:T(128)} %ids.1, s32[4]{0:T(128)} %bitcast.3, s32[8]{0:T(128)} %reshape.7.offs, f32[16]{0:T(128)} %weights.1, s32[24,4]{1,0:T(8,128)} %constant.18.clone.turns, f32[8,8,64,128]{3,2,1,0:T(8,128)} %receptor.1, f32[16,8,4913]{2,1,0:T(8,128)} %library.1, ...), custom_call_target="tpu_custom_call" | custom-call | tf_op jit(solution)/shard_map/consensus_density/pallas_call | solution.py:681
  62.0 1.5 %copy.19 = f32[8,16,128]{2,1,0:T(8,128)} copy(f32[8,16,128]{2,1,0:T(8,128)} %consensus_density.1) | data formatting | bytes 131072

commit v8 on v7

--- a/solution.py
+++ b/solution.py
@@ -333,7 +333,7 @@
     sum_ref[slot] = jnp.zeros((8, NY), F32)
     scale = 1.0 / (EXT * NZ * NY)
 
-    @pl.loop(0, 8, unroll=4)
+    @pl.loop(0, 8, unroll=True)
     def _(chunk):
         rows = pl.ds(pl.multiple_of(chunk * 8, 8), 8)
         fr = [work[k, rows, :NY] for k in range(KX)]

time: 63.7 us -> 63.5 us (level)
  no operation moved by 1% of the time
where the time goes in v8:
time: 63.5 us; the launch traced here: 63.3 us
  Pallas kernels  60.4 us (95%)
  local copies, waits for them, and re-layouts  2.83 us (4%)
    pallas_call x1, Pallas kernels, local(): pl.pallas_call(functools.partial(energy_kernel, slabs, probes, cells), in...  60.4 us
    unnamed x2, local copies, waits for them, and re-layouts  2.24 us

profile of v8, /device:TPU:1, one launch (start us, length us, event | category | flops | bytes accessed | tf_op | source)
XLA Modules:
  0.0 63.3 jit_solution(11015003753605551777)
XLA Ops:
  0.0 0.8 %copy.17 = s32[4,1,2]{2,0,1:T(4,128)S(1)} copy(s32[4,1,2]{0,2,1:T(2,128)} %param.19) | data formatting | bytes 64 | tf_op args[4]
  0.8 0.6 reshape.7.offs
  1.4 60.4 %consensus_density.1 = f32[8,16,128]{2,1,0:T(8,128)} custom-call(s32[4]{0:T(128)} %ids.1, s32[4]{0:T(128)} %bitcast.3, s32[8]{0:T(128)} %reshape.7.offs, f32[16]{0:T(128)} %weights.1, s32[24,4]{1,0:T(8,128)} %constant.18.clone.turns, f32[8,8,64,128]{3,2,1,0:T(8,128)} %receptor.1, f32[16,8,4913]{2,1,0:T(8,128)} %library.1, ...), custom_call_target="tpu_custom_call" | custom-call | tf_op jit(solution)/shard_map/consensus_density/pallas_call | solution.py:681
  61.8 1.5 %copy.19 = f32[8,16,128]{2,1,0:T(8,128)} copy(f32[8,16,128]{2,1,0:T(8,128)} %consensus_density.1) | data formatting | bytes 131072

commit v9 on v8

--- a/solution.py
+++ b/solution.py
@@ -333,7 +333,7 @@
     sum_ref[slot] = jnp.zeros((8, NY), F32)
     scale = 1.0 / (EXT * NZ * NY)
 
-    @pl.loop(0, 8, unroll=True)
+    @pl.loop(0, 8, unroll=2)
     def _(chunk):
         rows = pl.ds(pl.multiple_of(chunk * 8, 8), 8)
         fr = [work[k, rows, :NY] for k in range(KX)]

time: 63.5 us -> 63.8 us (level)
  no operation moved by 1% of the time
where the time goes in v9:
time: 63.8 us; the launch traced here: 63.6 us
  Pallas kernels  60.7 us (95%)
  local copies, waits for them, and re-layouts  2.83 us (4%)
    pallas_call x1, Pallas kernels, local(): pl.pallas_call(functools.partial(energy_kernel, slabs, probes, cells), in...  60.7 us
    unnamed x2, local copies, waits for them, and re-layouts  2.24 us

profile of v9, /device:TPU:1, one launch (start us, length us, event | category | flops | bytes accessed | tf_op | source)
XLA Modules:
  0.0 63.6 jit_solution(83981751580407909)
XLA Ops:
  0.0 0.8 %copy.17 = s32[4,1,2]{2,0,1:T(4,128)S(1)} copy(s32[4,1,2]{0,2,1:T(2,128)} %param.19) | data formatting | bytes 64 | tf_op args[4]
  0.8 0.6 reshape.7.offs
  1.4 60.7 %consensus_density.1 = f32[8,16,128]{2,1,0:T(8,128)} custom-call(s32[4]{0:T(128)} %ids.1, s32[4]{0:T(128)} %bitcast.3, s32[8]{0:T(128)} %reshape.7.offs, f32[16]{0:T(128)} %weights.1, s32[24,4]{1,0:T(8,128)} %constant.18.clone.turns, f32[8,8,64,128]{3,2,1,0:T(8,128)} %receptor.1, f32[16,8,4913]{2,1,0:T(8,128)} %library.1, ...), custom_call_target="tpu_custom_call" | custom-call | tf_op jit(solution)/shard_map/consensus_density/pallas_call | solution.py:681
  62.1 1.5 %copy.19 = f32[8,16,128]{2,1,0:T(8,128)} copy(f32[8,16,128]{2,1,0:T(8,128)} %consensus_density.1) | data formatting | bytes 131072
